TPU v7x, 512 devices: a whole 4x4x16 slice. The times are simulated.
512 devices in a mesh: blk: 64 (over z, y_hi, core), tensor: 8 (over y_lo, x).
Axes of the slice: x: 4, y: 4 (y_hi: 2, y_lo: 2; y = y_hi * 2 + y_lo), z: 16, core: 2. Of those that a mesh axis runs over, the one named last changes fastest.
Arguments:
- weights: bfloat16 [64, 2048, 1024], P('blk', None, 'tensor')
- grads: bfloat16 [64, 2048, 1024], P('blk', None, 'tensor'), may hold values from -6 to 6
- first_moment: float32 [64, 2048, 1024], P('blk', None, 'tensor'), may hold values from -6 to 6
- second_moment: float32 [64, 2048, 1024], P('blk', None, 'tensor'), may hold values from 0.02 to 2
- vectors: bfloat16 [64, 16, 1024], P('blk', None, 'tensor'), may hold values from -6 to 6
Outputs:
- new_weights: bfloat16 [64, 2048, 1024], P('blk', None, 'tensor')
- next_vectors: float32 [64, 16, 1024], P('blk', None, 'tensor')
All inputs are finite; a program needn't handle non-finite values.
Results may differ from a plain program's by a relative error of at most 0.004.
Values may be sent and summed in bfloat16 or wider, within the bound.
No kernel may reach another device: no remote copies, remote signals or barrier semaphores. Data moves between devices by JAX's collectives and lax.ppermute only.
A program may use at most 64 MiB of HBM per device.

v0:
```python
import jax
import jax.numpy as jnp
from jax import lax
from jax.sharding import PartitionSpec as P

learn_rate = 0.05
beta_one = 0.9
beta_two = 0.95
epsilon = 1e-08
decay_rate = 0.1
gossip_rate = 0.5
bias_one = 1.0 - 0.9**10
bias_two = 1.0 - 0.95**10


def shifted(value, axis, steps):
    count = lax.axis_size(axis)
    pairs = [(source, (source + steps) % count) for source in range(count)]
    return lax.ppermute(value, axis, pairs)


def gram_pair(left_block, right_block):
    return jnp.stack(
        [
            jnp.dot(left_block, left_block.T, precision=lax.Precision.HIGHEST),
            jnp.dot(right_block, right_block.T, precision=lax.Precision.HIGHEST),
        ]
    )


def normalize(block, gram):
    factor = jnp.linalg.cholesky(gram)
    return jax.scipy.linalg.solve_triangular(factor, block, lower=True)


def body(weights, grads, first_moment, second_moment, vectors):
    weight = weights[0]
    own_q = vectors[0]
    rank = own_q.shape[0]
    left_q = shifted(own_q, "blk", 1)
    both_q = jnp.concatenate([left_q, own_q], 0)
    partial_products = lax.dot_general(
        both_q, weight, (((1,), (1,)), ((), ())), preferred_element_type=jnp.float32
    )
    summed = lax.psum(partial_products, "tensor")
    from_left = shifted(summed[rank:], "blk", 1)
    from_right = shifted(summed[:rank], "blk", -1)
    diff_left = from_left - summed[:rank]
    diff_right = summed[rank:] - from_right
    grams = gram_pair(diff_left, diff_right)
    basis = jnp.concatenate(
        [normalize(diff_left, grams[0]), normalize(diff_right, grams[1])], 0
    ).astype(jnp.bfloat16)
    images = jnp.dot(basis, weight, preferred_element_type=jnp.float32)
    from_left_img = shifted(images[rank:], "blk", 1)
    from_right_img = shifted(images[:rank], "blk", -1)
    next_right = images[rank:] - from_right_img
    next_left = from_left_img - images[:rank]
    signed = jnp.concatenate(
        [basis[rank:].astype(jnp.float32), -basis[:rank].astype(jnp.float32)], 0
    )
    nexts = jnp.concatenate([next_right, next_left], 0)
    correction = lax.dot_general(
        signed, nexts, (((0,), (0,)), ((), ())), precision=lax.Precision.HIGHEST
    )
    wide = weight.astype(jnp.float32)
    gfull = grads[0].astype(jnp.float32)
    first = beta_one * first_moment[0] + (1.0 - beta_one) * gfull
    second = beta_two * second_moment[0] + (1.0 - beta_two) * gfull * gfull
    step = first / bias_one / (jnp.sqrt(second / bias_two) + epsilon) + decay_rate * wide
    updated = (wide - learn_rate * step - gossip_rate * correction).astype(jnp.bfloat16)
    return (updated[None], next_right[None])


def solution(mesh):
    return jax.shard_map(
        body,
        mesh=mesh,
        in_specs=(
            P("blk", None, "tensor"),
            P("blk", None, "tensor"),
            P("blk", None, "tensor"),
            P("blk", None, "tensor"),
            P("blk", None, "tensor"),
        ),
        out_specs=(P("blk", None, "tensor"), P("blk", None, "tensor")),
        check_vma=False,
    )
```

profile of v0, /device:TPU:4, one launch (start us, length us, event | category | flops | bytes accessed | tf_op | source)
XLA Modules:
  0.0 151.0 jit_solution(12044064934795575935)
XLA Ops:
  7.2 1.9 %collective-permute-start = (bf16[16,128]{1,0:T(8,128)(2,1)}, bf16[16,128]{1,0:T(8,128)(2,1)S(1)}, u32[]{:S(2)}, u32[]{:S(2)}) collective-permute-start(bf16[16,128]{1,0:T(8,128)(2,1)} %bitcast.40), channel_id=1, source_target_pairs={{0,8},{8,16},{16,24},{24,32},{32,40},{40,48},{48,56},{56,64},{64,7... | collective-permute-start | bytes 12296 | tf_op jit(solution)/shard_map/ppermute | solution.py:19
  9.1 13.0 %collective-permute-done = bf16[16,128]{1,0:T(8,128)(2,1)S(1)} collective-permute-done((bf16[16,128]{1,0:T(8,128)(2,1)}, bf16[16,128]{1,0:T(8,128)(2,1)S(1)}, u32[]{:S(2)}, u32[]{:S(2)}) %collective-permute-start) | collective-permute-done | bytes 4128 | tf_op jit(solution)/shard_map/ppermute | solution.py:19
  22.2 2.1 %fusion.14 = f32[32,2048]{1,0:T(8,128)} fusion(bf16[1,2048,128]{2,1,0:T(8,128)(2,1)} %param.8, bf16[16,128]{1,0:T(8,128)(2,1)} %bitcast.41, bf16[16,128]{1,0:T(8,128)(2,1)S(1)} %collective-permute-done), kind=kOutput, calls=%fused_computation.22 | convolution fusion | flops 16793600 | bytes 794624 | tf_op jit(solution)/shard_map/dot_general | solution.py:42
  24.3 84.3 %all-reduce.2.cloned.1.call-done = f32[32,2048]{1,0:T(8,128)} async-done(((f32[32,2048]{1,0:T(8,128)}), f32[32,2048]{1,0:T(8,128)}) %all-reduce.2.cloned.1.call-update) | async-done | bytes 262160 | tf_op jit(solution)/shard_map/psum | solution.py:45
  108.6 1.0 fusion.39
  109.7 2.9 %collective-permute-start.1 = (f32[16,2048]{1,0:T(8,128)S(1)}, f32[16,2048]{1,0:T(8,128)S(1)}, u32[]{:S(2)}, u32[]{:S(2)}) collective-permute-start(f32[16,2048]{1,0:T(8,128)S(1)} %get-tuple-element.4), channel_id=1, source_target_pairs={{0,504},{8,0},{16,8},{24,16},{32,24},{40,32},{48,40},{56,48},{64,5... | collective-permute-start | bytes 393224 | tf_op jit(solution)/shard_map/ppermute | solution.py:19
  112.6 1.9 %collective-permute-start.2 = (f32[16,2048]{1,0:T(8,128)S(1)}, f32[16,2048]{1,0:T(8,128)S(1)}, u32[]{:S(2)}, u32[]{:S(2)}) collective-permute-start(f32[16,2048]{1,0:T(8,128)S(1)} %get-tuple-element.5), channel_id=1, source_target_pairs={{0,8},{8,16},{16,24},{24,32},{32,40},{40,48},{48,56},{56,64},{64,7... | collective-permute-start | bytes 393224 | tf_op jit(solution)/shard_map/ppermute | solution.py:19
  114.5 0.6 collective-permute-done.1
  115.4 1.5 %cholesky.44 = f32[16,16]{1,0:T(8,128)S(1)} custom-call(f32[16,16]{1,0:T(8,128)S(1)} %fusion.33), custom_call_target="Cholesky" | custom-call | tf_op jit(solution)/shard_map/jit(cholesky)/cholesky | solution.py:32
  117.0 0.6 compare_reduce_fusion.1
  117.6 0.6 fusion.25
  118.3 1.2 custom-call.6
  119.5 3.2 %collective-permute-done.2 = f32[16,2048]{1,0:T(8,128)S(1)} collective-permute-done((f32[16,2048]{1,0:T(8,128)S(1)}, f32[16,2048]{1,0:T(8,128)S(1)}, u32[]{:S(2)}, u32[]{:S(2)}) %collective-permute-start.2) | collective-permute-done | bytes 131104 | tf_op jit(solution)/shard_map/ppermute | solution.py:19
  122.7 0.2 fusion.37
  123.1 1.5 cholesky.55
  124.6 0.6 compare_reduce_fusion
  125.2 0.6 fusion.26
  125.9 1.2 custom-call.7
  127.1 0.3 fusion.41
  127.5 0.3 convert_negate_fusion
  128.0 4.2 %collective-permute-start.3 = (f32[16,128]{1,0:T(8,128)S(1)}, f32[16,128]{1,0:T(8,128)S(1)}, u32[]{:S(2)}, u32[]{:S(2)}) collective-permute-start(f32[16,128]{1,0:T(8,128)S(1)} %get-tuple-element.8), channel_id=1, source_target_pairs={{0,504},{8,0},{16,8},{24,16},{32,24},{40,32},{48,40},{56,48},{64,5... | collective-permute-start | bytes 24584 | tf_op jit(solution)/shard_map/ppermute | solution.py:19
  132.2 1.9 %collective-permute-start.4 = (f32[16,128]{1,0:T(8,128)S(1)}, f32[16,128]{1,0:T(8,128)S(1)}, u32[]{:S(2)}, u32[]{:S(2)}) collective-permute-start(f32[16,128]{1,0:T(8,128)S(1)} %get-tuple-element.9), channel_id=1, source_target_pairs={{0,8},{8,16},{16,24},{24,32},{32,40},{40,48},{48,56},{56,64},{64,7... | collective-permute-start | bytes 24584 | tf_op jit(solution)/shard_map/ppermute | solution.py:19
  134.1 6.6 %collective-permute-done.4 = f32[16,128]{1,0:T(8,128)S(1)} collective-permute-done((f32[16,128]{1,0:T(8,128)S(1)}, f32[16,128]{1,0:T(8,128)S(1)}, u32[]{:S(2)}, u32[]{:S(2)}) %collective-permute-start.4) | collective-permute-done | bytes 8224 | tf_op jit(solution)/shard_map/ppermute | solution.py:19
  140.8 3.3 %fusion.2 = bf16[1,2048,128]{2,1,0:T(8,128)(2,1)} fusion(f32[1,2048,128]{2,1,0:T(8,128)S(1)} %copy-done.3, f32[1,2048,128]{2,1,0:T(8,128)S(1)} %copy-done.4, bf16[1,2048,128]{2,1,0:T(8,128)(2,1)S(1)} %copy-done.5, bf16[1,2048,128]{2,1,0:T(8,128)(2,1)S(1)} %copy-done.1, f32[16,2048]{1,0:T(8,128)S(1)} %get-tuple-element.10, ...), kind=kOutput, calls=%fused_computation.3 | convolution fusion | flops 105975808 | bytes 3948544 | tf_op jit(solution)/shard_map/dot_general | solution.py:63
  (25 shorter events, 0.8 us)
Async XLA Ops:
  7.2 101.5 %all-reduce.2.cloned.1.call-start = ((), (), s32[]{:S(2)}) async-start(), calls=%async_computation | async-start | bytes 524288 | tf_op jit(solution)/shard_map/psum | solution.py:45
  7.2 15.0 %collective-permute-start = (bf16[16,128]{1,0:T(8,128)(2,1)}, bf16[16,128]{1,0:T(8,128)(2,1)S(1)}, u32[]{:S(2)}, u32[]{:S(2)}) collective-permute-start(bf16[16,128]{1,0:T(8,128)(2,1)} %bitcast.40), channel_id=1, source_target_pairs={{0,8},{8,16},{16,24},{24,32},{32,40},{40,48},{48,56},{56,64},{64,7... | collective-permute-start | bytes 12296 | tf_op jit(solution)/shard_map/ppermute | solution.py:19
  22.2 118.6 %copy-start.4 = (f32[1,2048,128]{2,1,0:T(8,128)S(1)}, f32[1,2048,128]{2,1,0:T(8,128)}, u32[]{:S(2)}) copy-start(f32[1,2048,128]{2,1,0:T(8,128)} %param.10) | copy-start | bytes 3145732
  108.6 6.5 %copy-start = (f32[32,2048]{1,0:T(8,128)S(1)}, f32[32,2048]{1,0:T(8,128)}, u32[]{:S(2)}) copy-start(f32[32,2048]{1,0:T(8,128)} %all-reduce.2.cloned.1.call-done) | copy-start | bytes 786436
  109.7 5.4 %collective-permute-start.1 = (f32[16,2048]{1,0:T(8,128)S(1)}, f32[16,2048]{1,0:T(8,128)S(1)}, u32[]{:S(2)}, u32[]{:S(2)}) collective-permute-start(f32[16,2048]{1,0:T(8,128)S(1)} %get-tuple-element.4), channel_id=1, source_target_pairs={{0,504},{8,0},{16,8},{24,16},{32,24},{40,32},{48,40},{56,48},{64,5... | collective-permute-start | bytes 393224 | tf_op jit(solution)/shard_map/ppermute | solution.py:19
  112.6 10.1 %collective-permute-start.2 = (f32[16,2048]{1,0:T(8,128)S(1)}, f32[16,2048]{1,0:T(8,128)S(1)}, u32[]{:S(2)}, u32[]{:S(2)}) collective-permute-start(f32[16,2048]{1,0:T(8,128)S(1)} %get-tuple-element.5), channel_id=1, source_target_pairs={{0,8},{8,16},{16,24},{24,32},{32,40},{40,48},{48,56},{56,64},{64,7... | collective-permute-start | bytes 393224 | tf_op jit(solution)/shard_map/ppermute | solution.py:19
  115.1 25.7 %copy-start.3 = (f32[1,2048,128]{2,1,0:T(8,128)S(1)}, f32[1,2048,128]{2,1,0:T(8,128)}, u32[]{:S(2)}) copy-start(f32[1,2048,128]{2,1,0:T(8,128)} %param.11) | copy-start | bytes 3145732
  123.0 4.8 %copy-start.1 = (bf16[1,2048,128]{2,1,0:T(8,128)(2,1)S(1)}, bf16[1,2048,128]{2,1,0:T(8,128)(2,1)}, u32[]{:S(2)}) copy-start(bf16[1,2048,128]{2,1,0:T(8,128)(2,1)} %param.8) | copy-start | bytes 1572868
  127.5 13.4 %copy-start.5 = (bf16[1,2048,128]{2,1,0:T(8,128)(2,1)S(1)}, bf16[1,2048,128]{2,1,0:T(8,128)(2,1)}, u32[]{:S(2)}) copy-start(bf16[1,2048,128]{2,1,0:T(8,128)(2,1)} %param.9) | copy-start | bytes 1572868
  128.0 6.1 %collective-permute-start.3 = (f32[16,128]{1,0:T(8,128)S(1)}, f32[16,128]{1,0:T(8,128)S(1)}, u32[]{:S(2)}, u32[]{:S(2)}) collective-permute-start(f32[16,128]{1,0:T(8,128)S(1)} %get-tuple-element.8), channel_id=1, source_target_pairs={{0,504},{8,0},{16,8},{24,16},{32,24},{40,32},{48,40},{56,48},{64,5... | collective-permute-start | bytes 24584 | tf_op jit(solution)/shard_map/ppermute | solution.py:19
  132.2 8.6 %collective-permute-start.4 = (f32[16,128]{1,0:T(8,128)S(1)}, f32[16,128]{1,0:T(8,128)S(1)}, u32[]{:S(2)}, u32[]{:S(2)}) collective-permute-start(f32[16,128]{1,0:T(8,128)S(1)} %get-tuple-element.9), channel_id=1, source_target_pairs={{0,8},{8,16},{16,24},{24,32},{32,40},{40,48},{48,56},{56,64},{64,7... | collective-permute-start | bytes 24584 | tf_op jit(solution)/shard_map/ppermute | solution.py:19
  140.8 3.3 %copy-start.2 = (f32[16,128]{1,0:T(8,128)}, f32[16,128]{1,0:T(8,128)S(1)}, u32[]{:S(2)}) copy-start(f32[16,128]{1,0:T(8,128)S(1)} %get-tuple-element.6) | copy-start | bytes 24580
Sparse Core Ops, SparseCore 0:
  24.5 84.1 all-reduce.1
where the time goes:
time: 151 us
  waiting for transfers between devices  108 us (72%)
  between operations  14.2 us (9%)
  starting transfers between devices  12.9 us (9%)
  other arithmetic  8.1 us (5%)
  matrix products  6.73 us (4%)
    psum x1, waiting for transfers between devices, body(): summed = lax.psum(partial_products, 'tensor')  84.3 us
    ppermute x5, waiting for transfers between devices, shifted(): return lax.ppermute(value, axis, pairs)  23.5 us
    ppermute x5, starting transfers between devices, shifted(): return lax.ppermute(value, axis, pairs)  12.9 us
    another operation x6, other arithmetic, normalize(): factor = jnp.linalg.cholesky(gram)  4.33 us
    another operation x4, other arithmetic, normalize(): return jax.scipy.linalg.solve_triangular(factor, block, lower=True)  3.75 us
    dot_general x1, matrix products, body(): lax.dot_general(signed, nexts, (((0,), (0,)), ((), ())), precision=lax.Pr...  3.3 us
  transfers between devices with their start and end apart: 6, of which 5 were waited for; matrix products, arithmetic and copies ran while one was open for 3% of the time, Pallas kernels for 0%

commit v1 on v0

v1 whole, which is shorter than its diff:
```python
import jax
import jax.numpy as jnp
from jax import lax
from jax.experimental import pallas as pl
from jax.experimental.pallas import tpu as pltpu
from jax.sharding import PartitionSpec as P

learn_rate = 0.05
beta_one = 0.9
beta_two = 0.95
epsilon = 1e-08
decay_rate = 0.1
gossip_rate = 0.5
bias_one = 1.0 - 0.9**10
bias_two = 1.0 - 0.95**10

f32 = jnp.float32
bf16 = jnp.bfloat16


def dot(a, b, dims):
    return lax.dot_general(a, b, (dims, ((), ())), preferred_element_type=f32)


def swapped(value, axis, first):
    count = lax.axis_size(axis)
    pairs = []
    for low in range(first, first + count, 2):
        a, b = low % count, (low + 1) % count
        pairs += [(a, b), (b, a)]
    return lax.ppermute(value, axis, pairs)


def shifted(value, axis, steps):
    count = lax.axis_size(axis)
    pairs = [(source, (source + steps) % count) for source in range(count)]
    return lax.ppermute(value, axis, pairs)


def partial_kernel(w_ref, wa_ref, wb_ref, qa_ref, qb_ref, out_ref):
    qa, qb = qa_ref[...], qb_ref[...]
    zero = jnp.zeros_like(qa)
    lhs = jnp.concatenate(
        [
            jnp.concatenate([qa, -qa, zero], 1),
            jnp.concatenate([qb, zero, -qb], 1),
        ],
        0,
    )
    tile = 512
    for start in range(0, w_ref.shape[0], tile):
        rows = pl.ds(start, tile)
        rhs = jnp.concatenate([w_ref[rows], wa_ref[rows], wb_ref[rows]], 1)
        part = dot(lhs, rhs, ((1,), (1,))).astype(bf16)
        for copy in range(out_ref.shape[0]):
            out_ref[copy, :, rows] = part


def inverse_factor(gram_a, gram_b):
    rank = gram_a.shape[0]
    shape = (rank, 128)
    lane = lax.broadcasted_iota(jnp.int32, shape, 1)
    row = lax.broadcasted_iota(jnp.int32, shape, 0)
    is_a = (lane // rank) % 2 == 0
    left = []
    for j in range(rank):
        col_a = jnp.broadcast_to(gram_a[:, j : j + 1], shape)
        col_b = jnp.broadcast_to(gram_b[:, j : j + 1], shape)
        left.append(jnp.where(is_a, col_a, col_b))
    right = [jnp.where(row == j, 1.0, 0.0).astype(f32) for j in range(rank)]
    pivots = jnp.ones(shape, f32)
    for k in range(rank):
        pivot = jnp.broadcast_to(left[k][k : k + 1], shape)
        pivots = jnp.where(row == k, pivot, pivots)
        if k == rank - 1:
            break
        factor = jnp.where(row > k, left[k] / pivot, 0.0)
        for j in range(k + 1, rank):
            left[j] = left[j] - factor * jnp.broadcast_to(left[j][k : k + 1], shape)
        for j in range(k):
            right[j] = right[j] - factor * jnp.broadcast_to(right[j][k : k + 1], shape)
        right[k] = right[k] - factor
    gathered = jnp.zeros(shape, f32)
    for j in range(rank):
        gathered = jnp.where(lane % rank == j, right[j], gathered)
    return gathered / jnp.sqrt(pivots)


def finish_kernel(odd_ref, g_ref, w_ref, wa_ref, wb_ref, pre_ref, new_ref, next_ref):
    rank = next_ref.shape[0]
    diff = g_ref[0].astype(f32)
    for peer in range(1, g_ref.shape[0]):
        diff = diff + g_ref[peer].astype(f32)
    high = diff.astype(bf16)
    low = (diff - high.astype(f32)).astype(bf16)
    gram = (
        dot(high, high, ((1,), (1,)))
        + dot(high, low, ((1,), (1,)))
        + dot(low, high, ((1,), (1,)))
    )
    inverse = inverse_factor(gram[:rank, :rank], gram[rank:, rank : 2 * rank])
    lane = lax.broadcasted_iota(jnp.int32, inverse.shape, 1)
    is_a = (lane // rank) % 2 == 0
    coarse = inverse.astype(bf16).astype(f32)
    terms = jnp.where(lane < 4 * rank, coarse, inverse - coarse)
    mix = jnp.concatenate(
        [jnp.where(is_a, terms, 0.0), jnp.where(is_a, 0.0, terms)], 0
    ).astype(bf16)
    basis = dot(mix, jnp.concatenate([high, low, high, low], 0), ((1,), (0,))).astype(bf16)
    own = dot(basis, w_ref[...], ((1,), (0,)))
    next_a = own[:rank] - dot(basis[:rank], wa_ref[...], ((1,), (0,)))
    next_b = own[rank:] - dot(basis[rank:], wb_ref[...], ((1,), (0,)))
    next_ref[...] = jnp.where(odd_ref[0] == 1, next_b, next_a)
    nexts = jnp.concatenate([next_a, next_b], 0)
    one = nexts.astype(bf16)
    rest = nexts - one.astype(f32)
    two = rest.astype(bf16)
    three = (rest - two.astype(f32)).astype(bf16)
    nexts = jnp.concatenate([one, two, three], 0)
    tile = 512
    for start in range(0, w_ref.shape[0], tile):
        cols = basis[:, start : start + tile]
        lhs = jnp.concatenate([cols, cols, cols], 0)
        correction = dot(lhs, nexts, ((0,), (0,)))
        rows = pl.ds(start, tile)
        new_ref[rows] = (pre_ref[rows] - gossip_rate * correction).astype(bf16)


def body(weights, grads, first_moment, second_moment, vectors):
    weight = weights[0]
    own_q = vectors[0]
    rows, cols = weight.shape
    rank = own_q.shape[0]
    peers = lax.axis_size("tensor")
    odd = lax.axis_index("blk") % 2 == 1
    w_b = swapped(weight, "blk", 1)
    w_a = swapped(weight, "blk", 0)
    left_q = shifted(own_q, "blk", 1)
    q_a = jnp.where(odd, left_q, own_q)
    q_b = jnp.where(odd, own_q, left_q)

    wide = weight.astype(f32)
    gfull = grads[0].astype(f32)
    first = beta_one * first_moment[0] + (1.0 - beta_one) * gfull
    second = beta_two * second_moment[0] + (1.0 - beta_two) * gfull * gfull
    step = first / bias_one / (jnp.sqrt(second / bias_two) + epsilon) + decay_rate * wide
    pre = wide - learn_rate * step

    vmem = pl.BlockSpec(memory_space=pltpu.VMEM)
    params = pltpu.CompilerParams(vmem_limit_bytes=32 * 1024 * 1024)
    partials = pl.pallas_call(
        partial_kernel,
        out_shape=jax.ShapeDtypeStruct((peers, 2 * rank, rows), bf16),
        in_specs=[vmem] * 5,
        out_specs=vmem,
        compiler_params=params,
        name="partial_differences",
    )(weight, w_a, w_b, q_a, q_b)
    gathered = lax.all_to_all(partials, "tensor", 0, 0)
    new, next_right = pl.pallas_call(
        finish_kernel,
        out_shape=(
            jax.ShapeDtypeStruct((rows, cols), bf16),
            jax.ShapeDtypeStruct((rank, cols), f32),
        ),
        in_specs=[pl.BlockSpec(memory_space=pltpu.SMEM)] + [vmem] * 5,
        out_specs=(vmem, vmem),
        compiler_params=params,
        name="finish",
    )(odd.astype(jnp.int32)[None], gathered, weight, w_a, w_b, pre)
    return (new[None], next_right[None])


def solution(mesh):
    spec = P("blk", None, "tensor")
    return jax.shard_map(
        body,
        mesh=mesh,
        in_specs=(spec,) * 5,
        out_specs=(spec, spec),
        check_vma=False,
    )
```

time: 151 us -> 47.4 us (0.31)
  the two profiles are of different devices: /device:TPU:4 before, /device:TPU:2 now
where the time goes in v1:
time: 47.4 us; the launch traced here: 47 us
  starting transfers between devices  22.9 us (48%)
  waiting for transfers between devices  14.1 us (30%)
  Pallas kernels  3.92 us (8%)
  local copies, waits for them, and re-layouts  2.88 us (6%)
  other arithmetic  2.53 us (5%)
  between operations  0.7 us (1%)
    ppermute x2, starting transfers between devices, swapped(): return lax.ppermute(value, axis, pairs)  15.4 us
    all_to_all x1, waiting for transfers between devices, body(): gathered = lax.all_to_all(partials, 'tensor', 0, 0)  7.8 us
    ppermute x1, waiting for transfers between devices, shifted(): return lax.ppermute(value, axis, pairs)  6.31 us
    all_to_all x1, starting transfers between devices, body(): gathered = lax.all_to_all(partials, 'tensor', 0, 0)  5.08 us
    unnamed x10, local copies, waits for them, and re-layouts  2.88 us
    sub x1, other arithmetic, body(): pre = wide - learn_rate * step  2.53 us
    ppermute x1, starting transfers between devices, shifted(): return lax.ppermute(value, axis, pairs)  2.41 us
    pallas_call x1, Pallas kernels, body(): pl.pallas_call(finish_kernel, out_shape=(jax.ShapeDtypeStruct((rows, cols...  2.33 us
  transfers between devices with their start and end apart: 4, of which 2 were waited for; matrix products, arithmetic and copies ran while one was open for 5% of the time, Pallas kernels for 0%

profile of v1, /device:TPU:2, one launch (start us, length us, event | category | flops | bytes accessed | tf_op | source)
XLA Modules:
  0.0 47.0 jit_solution(3229629868013031770)
XLA Ops:
  0.6 13.5 %collective-permute-start.1 = (bf16[2048,128]{1,0:T(8,128)(2,1)}, bf16[2048,128]{1,0:T(8,128)(2,1)S(1)}, u32[]{:S(2)}, u32[]{:S(2)}) collective-permute-start(bf16[2048,128]{1,0:T(8,128)(2,1)} %bitcast.15), channel_id=1, source_target_pairs={{8,16},{16,8},{24,32},{32,24},{40,48},{48,40},{56,64},{64,56},{72,... | collective-permute-start | bytes 1572872 | tf_op jit(solution)/shard_map/ppermute | solution.py:31
  14.1 1.9 %collective-permute-start = (bf16[2048,128]{1,0:T(8,128)(2,1)}, bf16[2048,128]{1,0:T(8,128)(2,1)S(1)}, u32[]{:S(2)}, u32[]{:S(2)}) collective-permute-start(bf16[2048,128]{1,0:T(8,128)(2,1)} %bitcast.16), channel_id=1, source_target_pairs={{0,8},{8,0},{16,24},{24,16},{32,40},{40,32},{48,56},{56,48},{64,72... | collective-permute-start | bytes 1572872 | tf_op jit(solution)/shard_map/ppermute | solution.py:31
  16.0 2.4 %collective-permute-start.2 = (bf16[16,128]{1,0:T(8,128)(2,1)}, bf16[16,128]{1,0:T(8,128)(2,1)S(1)}, u32[]{:S(2)}, u32[]{:S(2)}) collective-permute-start(bf16[16,128]{1,0:T(8,128)(2,1)} %bitcast.19), channel_id=1, source_target_pairs={{0,8},{8,16},{16,24},{24,32},{32,40},{40,48},{48,56},{56,64},{64,7... | collective-permute-start | bytes 12296 | tf_op jit(solution)/shard_map/ppermute | solution.py:37
  18.5 0.0 copy-start.4
  18.5 6.3 %collective-permute-done.2 = bf16[16,128]{1,0:T(8,128)(2,1)S(1)} collective-permute-done((bf16[16,128]{1,0:T(8,128)(2,1)}, bf16[16,128]{1,0:T(8,128)(2,1)S(1)}, u32[]{:S(2)}, u32[]{:S(2)}) %collective-permute-start.2) | collective-permute-done | bytes 4128 | tf_op jit(solution)/shard_map/ppermute | solution.py:37
  24.8 0.0 copy-done.4
  24.8 0.0 collective-permute-done.1.wb_ref
  24.8 0.0 collective-permute-done.wa_ref
  24.8 0.0 copy-start
  24.8 1.0 %copy-done = bf16[1,2048,128]{2,1,0:T(8,128)(2,1)S(1)} copy-done((bf16[1,2048,128]{2,1,0:T(8,128)(2,1)S(1)}, bf16[1,2048,128]{2,1,0:T(8,128)(2,1)}, u32[]{:S(2)}) %copy-start) | copy-done | bytes 524312
  25.9 1.6 %partial_differences.1 = bf16[8,32,2048]{2,1,0:T(8,128)(2,1)} custom-call(bf16[2048,128]{1,0:T(8,128)(2,1)S(1)} %bitcast.17, bf16[2048,128]{1,0:T(8,128)(2,1)S(1)} %collective-permute-done.wa_ref, bf16[2048,128]{1,0:T(8,128)(2,1)S(1)} %collective-permute-done.1.wb_ref, bf16[16,128]{1,0:T(8,128)(2,1)S(1)} %get-tuple-element.7.qa_ref, ...), custom_call_target="tpu_custom_call" | custom-call | tf_op jit(solution)/shard_map/partial_differences/pallas_call | solution.py:151
  27.5 0.0 copy-start.2
  27.5 0.8 %copy-done.2 = bf16[2048,128]{1,0:T(8,128)(2,1)} copy-done((bf16[2048,128]{1,0:T(8,128)(2,1)}, bf16[2048,128]{1,0:T(8,128)(2,1)S(1)}, u32[]{:S(2)}) %copy-start.2) | copy-done | bytes 524312
  28.2 0.0 copy-start.1
  28.2 5.1 %all-to-all-start = ((bf16[8,32,2048]{2,1,0:T(8,128)(2,1)}), bf16[8,32,2048]{2,1,0:T(8,128)(2,1)S(1)}, u32[]{:S(2)}, u32[]{:S(2)}) async-start(bf16[8,32,2048]{2,1,0:T(8,128)(2,1)} %partial_differences.1), calls=%async_computation | async-start | bytes 2097152 | tf_op jit(solution)/shard_map/all_to_all | solution.py:159
  33.3 0.0 copy-done.1
  33.3 2.5 %convert_subtract_fusion.pre_ref = f32[2048,128]{1,0:T(8,128)S(1)} fusion(f32[1,2048,128]{2,1,0:T(8,128)} %param.8, f32[1,2048,128]{2,1,0:T(8,128)} %param.7, bf16[1,2048,128]{2,1,0:T(8,128)(2,1)} %param.6, bf16[1,2048,128]{2,1,0:T(8,128)(2,1)S(1)} %copy-done.1), kind=kLoop, calls=%fused_computation.3 | loop fusion | flops 4456448 | bytes 4194304 | tf_op jit(solution)/shard_map/sub | solution.py:147
  35.9 7.8 %all-to-all-done.g_ref = bf16[8,32,2048]{2,1,0:T(8,128)(2,1)S(1)} async-done(((bf16[8,32,2048]{2,1,0:T(8,128)(2,1)}), bf16[8,32,2048]{2,1,0:T(8,128)(2,1)S(1)}, u32[]{:S(2)}, u32[]{:S(2)}) %all-to-all-start) | async-done | bytes 1048608 | tf_op jit(solution)/shard_map/all_to_all | solution.py:159
  43.7 0.0 copy-start.3
  43.7 1.0 %copy-done.3 = bf16[2048,128]{1,0:T(8,128)(2,1)S(1)} copy-done((bf16[2048,128]{1,0:T(8,128)(2,1)S(1)}, bf16[2048,128]{1,0:T(8,128)(2,1)}, u32[]{:S(2)}) %copy-start.3) | copy-done | bytes 524312
  44.7 2.3 %finish.1 = (bf16[2048,128]{1,0:T(8,128)(2,1)}, f32[16,128]{1,0:T(8,128)}) custom-call(s32[1]{0:T(128)} %bitcast.odd_ref, bf16[8,32,2048]{2,1,0:T(8,128)(2,1)S(1)} %all-to-all-done.g_ref, bf16[2048,128]{1,0:T(8,128)(2,1)S(1)} %bitcast.18, bf16[2048,128]{1,0:T(8,128)(2,1)S(1)} %copy-done.3, bf16[2048,128]{1,0:T(8,128)(2,1)S(1)} %collective-permute-done.1.wb_ref, ...), custom_call_target="tpu_custom_call" | custom-call | tf_op jit(solution)/shard_map/finish/pallas_call | solution.py:160
  (1 shorter events, 0.0 us)
Async XLA Ops:
  0.6 24.2 %collective-permute-start.1 = (bf16[2048,128]{1,0:T(8,128)(2,1)}, bf16[2048,128]{1,0:T(8,128)(2,1)S(1)}, u32[]{:S(2)}, u32[]{:S(2)}) collective-permute-start(bf16[2048,128]{1,0:T(8,128)(2,1)} %bitcast.15), channel_id=1, source_target_pairs={{8,16},{16,8},{24,32},{32,24},{40,48},{48,40},{56,64},{64,56},{72,... | collective-permute-start | bytes 1572872 | tf_op jit(solution)/shard_map/ppermute | solution.py:31
  14.1 10.7 %collective-permute-start = (bf16[2048,128]{1,0:T(8,128)(2,1)}, bf16[2048,128]{1,0:T(8,128)(2,1)S(1)}, u32[]{:S(2)}, u32[]{:S(2)}) collective-permute-start(bf16[2048,128]{1,0:T(8,128)(2,1)} %bitcast.16), channel_id=1, source_target_pairs={{0,8},{8,0},{16,24},{24,16},{32,40},{40,32},{48,56},{56,48},{64,72... | collective-permute-start | bytes 1572872 | tf_op jit(solution)/shard_map/ppermute | solution.py:31
  16.0 8.8 %collective-permute-start.2 = (bf16[16,128]{1,0:T(8,128)(2,1)}, bf16[16,128]{1,0:T(8,128)(2,1)S(1)}, u32[]{:S(2)}, u32[]{:S(2)}) collective-permute-start(bf16[16,128]{1,0:T(8,128)(2,1)} %bitcast.19), channel_id=1, source_target_pairs={{0,8},{8,16},{16,24},{24,32},{32,40},{40,48},{48,56},{56,64},{64,7... | collective-permute-start | bytes 12296 | tf_op jit(solution)/shard_map/ppermute | solution.py:37
  18.5 6.3 %copy-start.4 = (bf16[1,16,128]{2,1,0:T(8,128)(2,1)S(1)}, bf16[1,16,128]{2,1,0:T(8,128)(2,1)}, u32[]{:S(2)}) copy-start(bf16[1,16,128]{2,1,0:T(8,128)(2,1)} %param.9) | copy-start | bytes 12292
  24.8 1.0 %copy-start = (bf16[1,2048,128]{2,1,0:T(8,128)(2,1)S(1)}, bf16[1,2048,128]{2,1,0:T(8,128)(2,1)}, u32[]{:S(2)}) copy-start(bf16[1,2048,128]{2,1,0:T(8,128)(2,1)} %param.5) | copy-start | bytes 1572868
  27.5 0.8 %copy-start.2 = (bf16[2048,128]{1,0:T(8,128)(2,1)}, bf16[2048,128]{1,0:T(8,128)(2,1)S(1)}, u32[]{:S(2)}) copy-start(bf16[2048,128]{1,0:T(8,128)(2,1)S(1)} %collective-permute-done.wa_ref) | copy-start | bytes 1572868
  28.2 5.1 %copy-start.1 = (bf16[1,2048,128]{2,1,0:T(8,128)(2,1)S(1)}, bf16[1,2048,128]{2,1,0:T(8,128)(2,1)}, u32[]{:S(2)}) copy-start(bf16[1,2048,128]{2,1,0:T(8,128)(2,1)} %param.5) | copy-start | bytes 1572868
  28.2 15.4 %all-to-all-start = ((bf16[8,32,2048]{2,1,0:T(8,128)(2,1)}), bf16[8,32,2048]{2,1,0:T(8,128)(2,1)S(1)}, u32[]{:S(2)}, u32[]{:S(2)}) async-start(bf16[8,32,2048]{2,1,0:T(8,128)(2,1)} %partial_differences.1), calls=%async_computation | async-start | bytes 2097152 | tf_op jit(solution)/shard_map/all_to_all | solution.py:159
  43.7 1.0 %copy-start.3 = (bf16[2048,128]{1,0:T(8,128)(2,1)S(1)}, bf16[2048,128]{1,0:T(8,128)(2,1)}, u32[]{:S(2)}) copy-start(bf16[2048,128]{1,0:T(8,128)(2,1)} %copy-done.2) | copy-start | bytes 1572868

commit v2 on v1

v2 whole, which is shorter than its diff:
```python
import jax
import jax.numpy as jnp
from jax import lax
from jax.experimental import pallas as pl
from jax.experimental.pallas import tpu as pltpu
from jax.sharding import PartitionSpec as P

learn_rate = 0.05
beta_one = 0.9
beta_two = 0.95
epsilon = 1e-08
decay_rate = 0.1
gossip_rate = 0.5
bias_one = 1.0 - 0.9**10
bias_two = 1.0 - 0.95**10

f32 = jnp.float32
bf16 = jnp.bfloat16


def dot(a, b, dims):
    return lax.dot_general(a, b, (dims, ((), ())), preferred_element_type=f32)


def shifted(value, axis, steps):
    count = lax.axis_size(axis)
    pairs = [(source, (source + steps) % count) for source in range(count)]
    return lax.ppermute(value, axis, pairs)


def product_kernel(w_hbm, q_hbm, pack_ref, w_ref, q_ref, sems):
    width, cols = w_ref.shape
    half = width // 2
    halves = [pl.ds(0, half), pl.ds(half, half)]
    copies = [pltpu.make_async_copy(q_hbm, q_ref, sems.at[2])]
    for i, rows in enumerate(halves):
        copies.append(pltpu.make_async_copy(w_hbm.at[rows], w_ref.at[rows], sems.at[i]))
    for copy in copies:
        copy.start()
    copies[0].wait()
    q = q_ref[...]
    pack_ref[:, pl.ds(width, cols)] = q.astype(f32)
    for i, rows in enumerate(halves):
        copies[i + 1].wait()
        pack_ref[:, rows] = dot(q, w_ref[rows], ((1,), (1,)))


def partial_kernel(pack_ref, w_ref, out_ref):
    width, cols = w_ref.shape
    q = pack_ref[:, pl.ds(width, cols)].astype(bf16)
    tile = 512
    for start in range(0, width, tile):
        rows = pl.ds(start, tile)
        w = w_ref[rows]
        part = (pack_ref[:, rows] - dot(q, w, ((1,), (1,)))).astype(bf16)
        for copy in range(out_ref.shape[0]):
            out_ref[copy, :, rows] = part


def inverse_factor(gram):
    rank = gram.shape[0]
    shape = (rank, 128)
    lane = lax.broadcasted_iota(jnp.int32, shape, 1)
    row = lax.broadcasted_iota(jnp.int32, shape, 0)
    left = [jnp.broadcast_to(gram[:, j : j + 1], shape) for j in range(rank)]
    right = [jnp.zeros(shape, f32) for j in range(rank)]
    pivots = jnp.ones(shape, f32)
    for k in range(rank):
        pivot = jnp.broadcast_to(left[k][k : k + 1], shape)
        pivots = jnp.where(row == k, pivot, pivots)
        right[k] = jnp.where(row == k, 1.0, 0.0).astype(f32)
        if k == rank - 1:
            break
        factor = jnp.where(row > k, left[k] / pivot, 0.0)
        for j in range(k + 1, rank):
            left[j] = left[j] - factor * jnp.broadcast_to(left[j][k : k + 1], shape)
        for j in range(k):
            right[j] = right[j] - factor * jnp.broadcast_to(right[j][k : k + 1], shape)
        right[k] = right[k] - factor
    gathered = jnp.zeros(shape, f32)
    for j in range(rank):
        gathered = jnp.where(lane % rank == j, right[j], gathered)
    return gathered / jnp.sqrt(pivots)


def basis_kernel(g_ref, basis_ref):
    rank = basis_ref.shape[0]
    diff = g_ref[0].astype(f32)
    for peer in range(1, g_ref.shape[0]):
        diff = diff + g_ref[peer].astype(f32)
    high = diff.astype(bf16)
    low = (diff - high.astype(f32)).astype(bf16)
    gram = (
        dot(high, high, ((1,), (1,)))
        + dot(high, low, ((1,), (1,)))
        + dot(low, high, ((1,), (1,)))
    )
    inverse = inverse_factor(gram)
    lane = lax.broadcasted_iota(jnp.int32, inverse.shape, 1)
    coarse = inverse.astype(bf16).astype(f32)
    mix = jnp.where(lane < 2 * rank, coarse, inverse - coarse)[:, : 4 * rank].astype(bf16)
    terms = jnp.concatenate([high, low, high, low], 0)
    basis_ref[...] = dot(mix, terms, ((1,), (0,))).astype(bf16)


def image_kernel(basis_ref, wl_ref, w_ref, pack_ref):
    width, cols = w_ref.shape
    basis = basis_ref[...]
    pack_ref[:, :width] = basis
    image = dot(basis, wl_ref[...], ((1,), (0,))) - dot(basis, w_ref[...], ((1,), (0,)))
    for term in range(3):
        piece = image.astype(bf16)
        pack_ref[:, pl.ds(width + term * cols, cols)] = piece
        image = image - piece.astype(f32)


def update_kernel(left_ref, right_ref, pre_ref, new_hbm, next_hbm, new_ref, next_ref, sems):
    width, cols = new_ref.shape
    terms = [pl.ds(width + term * cols, cols) for term in range(3)]
    pieces = [right_ref[:, t] for t in terms]
    next_ref[...] = (
        pieces[0].astype(f32) + pieces[1].astype(f32) + pieces[2].astype(f32)
    )
    copies = [pltpu.make_async_copy(next_ref, next_hbm, sems.at[0])]
    copies[0].start()
    nexts = jnp.concatenate(pieces + [-left_ref[:, t] for t in terms], 0)
    tile = 512
    for start in range(0, width, tile):
        rows = pl.ds(start, tile)
        left, right = left_ref[:, rows], right_ref[:, rows]
        lhs = jnp.concatenate([right, right, right, left, left, left], 0)
        correction = dot(lhs, nexts, ((0,), (0,)))
        new_ref[rows] = (pre_ref[rows] - gossip_rate * correction).astype(bf16)
        copies.append(
            pltpu.make_async_copy(new_ref.at[rows], new_hbm.at[rows], sems.at[len(copies)])
        )
        copies[-1].start()
    for copy in copies:
        copy.wait()


def body(weights, grads, first_moment, second_moment, vectors):
    weight = weights[0]
    rows, cols = weight.shape
    rank = vectors.shape[1]
    peers = lax.axis_size("tensor")
    vmem = pl.BlockSpec(memory_space=pltpu.VMEM)
    hbm = pl.BlockSpec(memory_space=pltpu.HBM)
    shaped = jax.ShapeDtypeStruct

    def call(kernel, name, out_shape, *operands):
        return pl.pallas_call(
            kernel,
            out_shape=out_shape,
            in_specs=[vmem] * len(operands),
            out_specs=jax.tree.map(lambda _: vmem, out_shape),
            compiler_params=pltpu.CompilerParams(vmem_limit_bytes=8 * 1024 * 1024),
            cost_estimate=pl.CostEstimate(
                flops=10_000_000, bytes_accessed=4_000_000, transcendentals=500_000
            ),
            name=name,
        )(*operands)

    product, w_here = pl.pallas_call(
        product_kernel,
        out_shape=(shaped((rank, rows + cols), f32), shaped((rows, cols), bf16)),
        in_specs=[hbm, hbm],
        out_specs=(vmem, vmem),
        scratch_shapes=[pltpu.VMEM((rank, cols), bf16), pltpu.SemaphoreType.DMA((3,))],
        compiler_params=pltpu.CompilerParams(vmem_limit_bytes=8 * 1024 * 1024),
        cost_estimate=pl.CostEstimate(
            flops=10_000_000, bytes_accessed=4_000_000, transcendentals=0
        ),
        name="own_product",
    )(
        pltpu.with_memory_space_constraint(weight, pltpu.HBM),
        pltpu.with_memory_space_constraint(vectors[0], pltpu.HBM),
    )
    left_product = shifted(product, "blk", 1)
    w_left = shifted(weight, "blk", 1)
    partials = call(
        partial_kernel,
        "partial_differences",
        shaped((peers, rank, rows), bf16),
        left_product,
        w_here,
    )
    gathered = lax.all_to_all(partials, "tensor", 0, 0)
    basis = call(basis_kernel, "basis", shaped((rank, rows), bf16), gathered)
    pack = call(
        image_kernel, "image", shaped((rank, rows + 3 * cols), bf16), basis, w_left, w_here
    )
    right_pack = shifted(pack, "blk", -1)

    wide = w_here.astype(f32)
    gfull = grads[0].astype(f32)
    first = beta_one * first_moment[0] + (1.0 - beta_one) * gfull
    second = beta_two * second_moment[0] + (1.0 - beta_two) * gfull * gfull
    step = first / bias_one / (jnp.sqrt(second / bias_two) + epsilon) + decay_rate * wide
    pre = wide - learn_rate * step

    new, next_right = pl.pallas_call(
        update_kernel,
        out_shape=(shaped((rows, cols), bf16), shaped((rank, cols), f32)),
        in_specs=[vmem] * 3,
        out_specs=(hbm, hbm),
        scratch_shapes=[
            pltpu.VMEM((rows, cols), bf16),
            pltpu.VMEM((rank, cols), f32),
            pltpu.SemaphoreType.DMA((1 + rows // 512,)),
        ],
        compiler_params=pltpu.CompilerParams(vmem_limit_bytes=8 * 1024 * 1024),
        cost_estimate=pl.CostEstimate(
            flops=10_000_000, bytes_accessed=4_000_000, transcendentals=0
        ),
        name="update",
    )(pack, right_pack, pre)
    return (new[None], next_right[None])


def solution(mesh):
    spec = P("blk", None, "tensor")
    return jax.shard_map(
        body,
        mesh=mesh,
        in_specs=(spec,) * 5,
        out_specs=(spec, spec),
        check_vma=False,
    )
```

time: 47.4 us -> 38.6 us (0.81)
  the two profiles are of different devices: /device:TPU:2 before, /device:TPU:1 now
where the time goes in v2:
time: 38.6 us; the launch traced here: 38.3 us
  starting transfers between devices  21 us (54%)
  blocking collectives  10.5 us (27%)
  Pallas kernels  3.76 us (10%)
  waiting for transfers between devices  1.48 us (4%)
  other arithmetic  0.87 us (2%)
  between operations  0.74 us (2%)
    ppermute x3, starting transfers between devices, shifted(): return lax.ppermute(value, axis, pairs)  21 us
    all_to_all x1, blocking collectives, body(): gathered = lax.all_to_all(partials, 'tensor', 0, 0)  10.5 us
    ppermute x3, waiting for transfers between devices, shifted(): return lax.ppermute(value, axis, pairs)  1.48 us
    pallas_call x1, Pallas kernels, body(): pl.pallas_call(product_kernel, out_shape=(shaped((rank, rows + cols), f32...  1.42 us
    pallas_call x3, Pallas kernels, call(): pl.pallas_call(kernel, out_shape=out_shape, in_specs=[vmem] * len(operand...  1.25 us
    pallas_call x1, Pallas kernels, body(): pl.pallas_call(update_kernel, out_shape=(shaped((rows, cols), bf16), shap...  1.09 us
    sub x1, other arithmetic, body(): pre = wide - learn_rate * step  0.87 us
  transfers between devices with their start and end apart: 3, of which 1 were waited for; matrix products, arithmetic and copies ran while one was open for 2% of the time, Pallas kernels for 3%

profile of v2, /device:TPU:1, one launch (start us, length us, event | category | flops | bytes accessed | tf_op | source)
XLA Modules:
  0.0 38.3 jit_solution(5696034839270396542)
XLA Ops:
  0.6 0.0 copy-start.2
  0.6 1.4 %own_product.1 = (f32[16,2176]{1,0:T(8,128)S(1)}, bf16[2048,128]{1,0:T(8,128)(2,1)S(1)}) custom-call(bf16[2048,128]{1,0:T(8,128)(2,1)} %bitcast.11, bf16[16,128]{1,0:T(8,128)(2,1)} %bitcast.13), custom_call_target="tpu_custom_call" | custom-call | flops 10000000 | bytes 4000000 | tf_op jit(solution)/shard_map/own_product/pallas_call | solution.py:164
  2.1 6.2 %collective-permute-start = (f32[16,2176]{1,0:T(8,128)S(1)}, f32[16,2176]{1,0:T(8,128)S(1)}, u32[]{:S(2)}, u32[]{:S(2)}) collective-permute-start(f32[16,2176]{1,0:T(8,128)S(1)} %get-tuple-element.6), channel_id=1, source_target_pairs={{0,8},{8,16},{16,24},{24,32},{32,40},{40,48},{48,56},{56,64},{64,7... | collective-permute-start | bytes 417800 | tf_op jit(solution)/shard_map/ppermute | solution.py:28
  8.3 0.0 copy-done.2
  8.3 1.9 %collective-permute-start.1 = (bf16[2048,128]{1,0:T(8,128)(2,1)S(1)}, bf16[2048,128]{1,0:T(8,128)(2,1)S(1)}, u32[]{:S(2)}, u32[]{:S(2)}) collective-permute-start(bf16[2048,128]{1,0:T(8,128)(2,1)S(1)} %bitcast.12), channel_id=1, source_target_pairs={{0,8},{8,16},{16,24},{24,32},{32,40},{40,48},{48,56},{56,64},{64,7... | collective-permute-start | bytes 1572872 | tf_op jit(solution)/shard_map/ppermute | solution.py:28
  10.2 1.5 %collective-permute-done.pack_ref = f32[16,2176]{1,0:T(8,128)S(1)} collective-permute-done((f32[16,2176]{1,0:T(8,128)S(1)}, f32[16,2176]{1,0:T(8,128)S(1)}, u32[]{:S(2)}, u32[]{:S(2)}) %collective-permute-start) | collective-permute-done | bytes 139296 | tf_op jit(solution)/shard_map/ppermute | solution.py:28
  11.7 0.3 partial_differences.1
  12.0 0.0 copy-start.3
  12.0 10.5 %all_to_all.5.g_ref = bf16[8,16,2048]{2,1,0:T(8,128)(2,1)S(1)} all-to-all(bf16[8,16,2048]{2,1,0:T(8,128)(2,1)S(1)} %partial_differences.1), channel_id=1, replica_groups=mesh['blk'=64,'tensor'=8] {'tensor'}, dimensions={0} | all-to-all | bytes 1048576 | tf_op jit(solution)/shard_map/all_to_all | solution.py:188
  22.5 0.0 copy-start
  22.5 0.0 copy-start.1
  22.5 0.7 %basis.1.basis_ref = bf16[16,2048]{1,0:T(8,128)(2,1)S(1)} custom-call(bf16[8,16,2048]{2,1,0:T(8,128)(2,1)S(1)} %all_to_all.5.g_ref), custom_call_target="tpu_custom_call" | custom-call | flops 10000000 | bytes 4000000 | tf_op jit(solution)/shard_map/basis/pallas_call | solution.py:152
  23.2 0.0 collective-permute-done.1.wl_ref
  23.2 0.3 image.1.left_ref
  23.5 12.8 %collective-permute-start.2 = (bf16[16,2432]{1,0:T(8,128)(2,1)S(1)}, bf16[16,2432]{1,0:T(8,128)(2,1)S(1)}, u32[]{:S(2)}, u32[]{:S(2)}) collective-permute-start(bf16[16,2432]{1,0:T(8,128)(2,1)S(1)} %image.1.left_ref), channel_id=1, source_target_pairs={{0,504},{8,0},{16,8},{24,16},{32,24},{40,32},{48,40},{56,48},{64,5... | collective-permute-start | bytes 233480 | tf_op jit(solution)/shard_map/ppermute | solution.py:28
  36.3 0.0 copy-done.3
  36.3 0.0 copy-done
  36.3 0.0 copy-done.1
  36.4 0.9 %convert_subtract_fusion.pre_ref = f32[2048,128]{1,0:T(8,128)S(1)} fusion(bf16[2048,128]{1,0:T(8,128)(2,1)S(1)} %get-tuple-element.7.w_ref, f32[1,2048,128]{2,1,0:T(8,128)S(1)} %copy-done, f32[1,2048,128]{2,1,0:T(8,128)S(1)} %copy-done.1, bf16[1,2048,128]{2,1,0:T(8,128)(2,1)S(1)} %copy-done.3), kind=kLoop, calls=%fused_computation.3 | loop fusion | flops 4456448 | bytes 4194304 | tf_op jit(solution)/shard_map/sub | solution.py:200
  37.2 0.0 collective-permute-done.2.right_ref
  37.2 1.1 %update.1 = (bf16[2048,128]{1,0:T(8,128)(2,1)}, f32[16,128]{1,0:T(8,128)}) custom-call(bf16[16,2432]{1,0:T(8,128)(2,1)S(1)} %image.1.left_ref, bf16[16,2432]{1,0:T(8,128)(2,1)S(1)} %collective-permute-done.2.right_ref, f32[2048,128]{1,0:T(8,128)S(1)} %convert_subtract_fusion.pre_ref), custom_call_target="tpu_custom_call" | custom-call | flops 10000000 | bytes 4000000 | tf_op jit(solution)/shard_map/update/pallas_call | solution.py:202
Async XLA Ops:
  0.6 7.7 %copy-start.2 = (bf16[1,2048,128]{2,1,0:T(8,128)(2,1)S(1)}, bf16[1,2048,128]{2,1,0:T(8,128)(2,1)}, u32[]{:S(2)}) copy-start(bf16[1,2048,128]{2,1,0:T(8,128)(2,1)} %param.5) | copy-start | bytes 1572868
  2.1 9.6 %collective-permute-start = (f32[16,2176]{1,0:T(8,128)S(1)}, f32[16,2176]{1,0:T(8,128)S(1)}, u32[]{:S(2)}, u32[]{:S(2)}) collective-permute-start(f32[16,2176]{1,0:T(8,128)S(1)} %get-tuple-element.6), channel_id=1, source_target_pairs={{0,8},{8,16},{16,24},{24,32},{32,40},{40,48},{48,56},{56,64},{64,7... | collective-permute-start | bytes 417800 | tf_op jit(solution)/shard_map/ppermute | solution.py:28
  8.3 14.9 %collective-permute-start.1 = (bf16[2048,128]{1,0:T(8,128)(2,1)S(1)}, bf16[2048,128]{1,0:T(8,128)(2,1)S(1)}, u32[]{:S(2)}, u32[]{:S(2)}) collective-permute-start(bf16[2048,128]{1,0:T(8,128)(2,1)S(1)} %bitcast.12), channel_id=1, source_target_pairs={{0,8},{8,16},{16,24},{24,32},{32,40},{40,48},{48,56},{56,64},{64,7... | collective-permute-start | bytes 1572872 | tf_op jit(solution)/shard_map/ppermute | solution.py:28
  12.0 24.4 %copy-start.3 = (bf16[1,2048,128]{2,1,0:T(8,128)(2,1)S(1)}, bf16[1,2048,128]{2,1,0:T(8,128)(2,1)}, u32[]{:S(2)}) copy-start(bf16[1,2048,128]{2,1,0:T(8,128)(2,1)} %param.6) | copy-start | bytes 1572868
  22.5 13.9 %copy-start = (f32[1,2048,128]{2,1,0:T(8,128)S(1)}, f32[1,2048,128]{2,1,0:T(8,128)}, u32[]{:S(2)}) copy-start(f32[1,2048,128]{2,1,0:T(8,128)} %param.8) | copy-start | bytes 3145732
  22.5 13.9 %copy-start.1 = (f32[1,2048,128]{2,1,0:T(8,128)S(1)}, f32[1,2048,128]{2,1,0:T(8,128)}, u32[]{:S(2)}) copy-start(f32[1,2048,128]{2,1,0:T(8,128)} %param.7) | copy-start | bytes 3145732
  23.5 13.7 %collective-permute-start.2 = (bf16[16,2432]{1,0:T(8,128)(2,1)S(1)}, bf16[16,2432]{1,0:T(8,128)(2,1)S(1)}, u32[]{:S(2)}, u32[]{:S(2)}) collective-permute-start(bf16[16,2432]{1,0:T(8,128)(2,1)S(1)} %image.1.left_ref), channel_id=1, source_target_pairs={{0,504},{8,0},{16,8},{24,16},{32,24},{40,32},{48,40},{56,48},{64,5... | collective-permute-start | bytes 233480 | tf_op jit(solution)/shard_map/ppermute | solution.py:28

commit v3 on v2

--- a/solution.py
+++ b/solution.py
@@ -30,31 +30,23 @@
 
 def product_kernel(w_hbm, q_hbm, pack_ref, w_ref, q_ref, sems):
     width, cols = w_ref.shape
-    half = width // 2
-    halves = [pl.ds(0, half), pl.ds(half, half)]
-    copies = [pltpu.make_async_copy(q_hbm, q_ref, sems.at[2])]
-    for i, rows in enumerate(halves):
-        copies.append(pltpu.make_async_copy(w_hbm.at[rows], w_ref.at[rows], sems.at[i]))
-    for copy in copies:
-        copy.start()
-    copies[0].wait()
+    w_copy = pltpu.make_async_copy(w_hbm, w_ref, sems.at[0])
+    q_copy = pltpu.make_async_copy(q_hbm, q_ref, sems.at[1])
+    w_copy.start()
+    q_copy.start()
+    q_copy.wait()
     q = q_ref[...]
     pack_ref[:, pl.ds(width, cols)] = q.astype(f32)
-    for i, rows in enumerate(halves):
-        copies[i + 1].wait()
-        pack_ref[:, rows] = dot(q, w_ref[rows], ((1,), (1,)))
+    w_copy.wait()
+    pack_ref[:, :width] = dot(q, w_ref[...], ((1,), (1,)))
 
 
 def partial_kernel(pack_ref, w_ref, out_ref):
     width, cols = w_ref.shape
     q = pack_ref[:, pl.ds(width, cols)].astype(bf16)
-    tile = 512
-    for start in range(0, width, tile):
-        rows = pl.ds(start, tile)
-        w = w_ref[rows]
-        part = (pack_ref[:, rows] - dot(q, w, ((1,), (1,)))).astype(bf16)
-        for copy in range(out_ref.shape[0]):
-            out_ref[copy, :, rows] = part
+    part = (pack_ref[:, :width] - dot(q, w_ref[...], ((1,), (1,)))).astype(bf16)
+    for copy in range(out_ref.shape[0]):
+        out_ref[copy] = part
 
 
 def inverse_factor(gram):
@@ -163,10 +155,13 @@
 
     product, w_here = pl.pallas_call(
         product_kernel,
-        out_shape=(shaped((rank, rows + cols), f32), shaped((rows, cols), bf16)),
+        out_shape=(
+            pltpu.VMEM((rank, rows + cols), f32),
+            pltpu.VMEM((rows, cols), bf16),
+        ),
         in_specs=[hbm, hbm],
         out_specs=(vmem, vmem),
-        scratch_shapes=[pltpu.VMEM((rank, cols), bf16), pltpu.SemaphoreType.DMA((3,))],
+        scratch_shapes=[pltpu.VMEM((rank, cols), bf16), pltpu.SemaphoreType.DMA((2,))],
         compiler_params=pltpu.CompilerParams(vmem_limit_bytes=8 * 1024 * 1024),
         cost_estimate=pl.CostEstimate(
             flops=10_000_000, bytes_accessed=4_000_000, transcendentals=0
@@ -177,7 +172,7 @@
         pltpu.with_memory_space_constraint(vectors[0], pltpu.HBM),
     )
     left_product = shifted(product, "blk", 1)
-    w_left = shifted(weight, "blk", 1)
+    w_left = shifted(w_here, "blk", 1)
     partials = call(
         partial_kernel,
         "partial_differences",

time: 38.6 us -> 38.5 us (level)
  no operation moved by 1% of the time
where the time goes in v3:
time: 38.5 us; the launch traced here: 38.2 us
  starting transfers between devices  21 us (55%)
  blocking collectives  10.5 us (27%)
  Pallas kernels  3.65 us (9%)
  waiting for transfers between devices  1.49 us (4%)
  other arithmetic  0.87 us (2%)
  between operations  0.73 us (2%)
    ppermute x3, starting transfers between devices, shifted(): return lax.ppermute(value, axis, pairs)  21 us
    all_to_all x1, blocking collectives, body(): gathered = lax.all_to_all(partials, 'tensor', 0, 0)  10.5 us
    ppermute x3, waiting for transfers between devices, shifted(): return lax.ppermute(value, axis, pairs)  1.49 us
    pallas_call x1, Pallas kernels, body(): pl.pallas_call(product_kernel, out_shape=(pltpu.VMEM((rank, rows + cols),...  1.31 us
    pallas_call x3, Pallas kernels, call(): pl.pallas_call(kernel, out_shape=out_shape, in_specs=[vmem] * len(operand...  1.25 us
    pallas_call x1, Pallas kernels, body(): pl.pallas_call(update_kernel, out_shape=(shaped((rows, cols), bf16), shap...  1.09 us
    sub x1, other arithmetic, body(): pre = wide - learn_rate * step  0.87 us
  transfers between devices with their start and end apart: 3, of which 1 were waited for; matrix products, arithmetic and copies ran while one was open for 2% of the time, Pallas kernels for 3%

profile of v3, /device:TPU:1, one launch (start us, length us, event | category | flops | bytes accessed | tf_op | source)
XLA Modules:
  0.0 38.2 jit_solution(11167196739380819293)
XLA Ops:
  0.6 1.3 %own_product.1 = (f32[16,2176]{1,0:T(8,128)S(1)}, bf16[2048,128]{1,0:T(8,128)(2,1)S(1)}) custom-call(bf16[2048,128]{1,0:T(8,128)(2,1)} %bitcast.11, bf16[16,128]{1,0:T(8,128)(2,1)} %bitcast.12), custom_call_target="tpu_custom_call" | custom-call | flops 10000000 | bytes 4000000 | tf_op jit(solution)/shard_map/own_product/pallas_call | solution.py:156
  1.9 6.2 %collective-permute-start = (f32[16,2176]{1,0:T(8,128)S(1)}, f32[16,2176]{1,0:T(8,128)S(1)}, u32[]{:S(2)}, u32[]{:S(2)}) collective-permute-start(f32[16,2176]{1,0:T(8,128)S(1)} %get-tuple-element.6), channel_id=1, source_target_pairs={{0,8},{8,16},{16,24},{24,32},{32,40},{40,48},{48,56},{56,64},{64,7... | collective-permute-start | bytes 417800 | tf_op jit(solution)/shard_map/ppermute | solution.py:28
  8.2 1.9 %collective-permute-start.1 = (bf16[2048,128]{1,0:T(8,128)(2,1)S(1)}, bf16[2048,128]{1,0:T(8,128)(2,1)S(1)}, u32[]{:S(2)}, u32[]{:S(2)}) collective-permute-start(bf16[2048,128]{1,0:T(8,128)(2,1)S(1)} %get-tuple-element.7.w_ref), channel_id=1, source_target_pairs={{0,8},{8,16},{16,24},{24,32},{32,40},{40,48},{48,56},{56,64},{64,7... | collective-permute-start | bytes 1572872 | tf_op jit(solution)/shard_map/ppermute | solution.py:28
  10.1 1.5 %collective-permute-done.pack_ref = f32[16,2176]{1,0:T(8,128)S(1)} collective-permute-done((f32[16,2176]{1,0:T(8,128)S(1)}, f32[16,2176]{1,0:T(8,128)S(1)}, u32[]{:S(2)}, u32[]{:S(2)}) %collective-permute-start) | collective-permute-done | bytes 139296 | tf_op jit(solution)/shard_map/ppermute | solution.py:28
  11.6 0.3 partial_differences.1
  11.8 0.0 copy-start.2
  11.9 10.5 %all_to_all.5.g_ref = bf16[8,16,2048]{2,1,0:T(8,128)(2,1)S(1)} all-to-all(bf16[8,16,2048]{2,1,0:T(8,128)(2,1)S(1)} %partial_differences.1), channel_id=1, replica_groups=mesh['blk'=64,'tensor'=8] {'tensor'}, dimensions={0} | all-to-all | bytes 1048576 | tf_op jit(solution)/shard_map/all_to_all | solution.py:183
  22.3 0.0 copy-start
  22.3 0.0 copy-start.1
  22.3 0.7 %basis.1.basis_ref = bf16[16,2048]{1,0:T(8,128)(2,1)S(1)} custom-call(bf16[8,16,2048]{2,1,0:T(8,128)(2,1)S(1)} %all_to_all.5.g_ref), custom_call_target="tpu_custom_call" | custom-call | flops 10000000 | bytes 4000000 | tf_op jit(solution)/shard_map/basis/pallas_call | solution.py:144
  23.1 0.0 collective-permute-done.1.wl_ref
  23.1 0.3 image.1.left_ref
  23.4 12.8 %collective-permute-start.2 = (bf16[16,2432]{1,0:T(8,128)(2,1)S(1)}, bf16[16,2432]{1,0:T(8,128)(2,1)S(1)}, u32[]{:S(2)}, u32[]{:S(2)}) collective-permute-start(bf16[16,2432]{1,0:T(8,128)(2,1)S(1)} %image.1.left_ref), channel_id=1, source_target_pairs={{0,504},{8,0},{16,8},{24,16},{32,24},{40,32},{48,40},{56,48},{64,5... | collective-permute-start | bytes 233480 | tf_op jit(solution)/shard_map/ppermute | solution.py:28
  36.2 0.0 copy-done.2
  36.2 0.0 copy-done
  36.2 0.0 copy-done.1
  36.2 0.9 %convert_subtract_fusion.pre_ref = f32[2048,128]{1,0:T(8,128)S(1)} fusion(bf16[2048,128]{1,0:T(8,128)(2,1)S(1)} %get-tuple-element.7.w_ref, f32[1,2048,128]{2,1,0:T(8,128)S(1)} %copy-done, f32[1,2048,128]{2,1,0:T(8,128)S(1)} %copy-done.1, bf16[1,2048,128]{2,1,0:T(8,128)(2,1)S(1)} %copy-done.2), kind=kLoop, calls=%fused_computation.3 | loop fusion | flops 4456448 | bytes 4194304 | tf_op jit(solution)/shard_map/sub | solution.py:195
  37.1 0.0 collective-permute-done.2.right_ref
  37.1 1.1 %update.1 = (bf16[2048,128]{1,0:T(8,128)(2,1)}, f32[16,128]{1,0:T(8,128)}) custom-call(bf16[16,2432]{1,0:T(8,128)(2,1)S(1)} %image.1.left_ref, bf16[16,2432]{1,0:T(8,128)(2,1)S(1)} %collective-permute-done.2.right_ref, f32[2048,128]{1,0:T(8,128)S(1)} %convert_subtract_fusion.pre_ref), custom_call_target="tpu_custom_call" | custom-call | flops 10000000 | bytes 4000000 | tf_op jit(solution)/shard_map/update/pallas_call | solution.py:197
Async XLA Ops:
  1.9 9.6 %collective-permute-start = (f32[16,2176]{1,0:T(8,128)S(1)}, f32[16,2176]{1,0:T(8,128)S(1)}, u32[]{:S(2)}, u32[]{:S(2)}) collective-permute-start(f32[16,2176]{1,0:T(8,128)S(1)} %get-tuple-element.6), channel_id=1, source_target_pairs={{0,8},{8,16},{16,24},{24,32},{32,40},{40,48},{48,56},{56,64},{64,7... | collective-permute-start | bytes 417800 | tf_op jit(solution)/shard_map/ppermute | solution.py:28
  8.2 14.9 %collective-permute-start.1 = (bf16[2048,128]{1,0:T(8,128)(2,1)S(1)}, bf16[2048,128]{1,0:T(8,128)(2,1)S(1)}, u32[]{:S(2)}, u32[]{:S(2)}) collective-permute-start(bf16[2048,128]{1,0:T(8,128)(2,1)S(1)} %get-tuple-element.7.w_ref), channel_id=1, source_target_pairs={{0,8},{8,16},{16,24},{24,32},{32,40},{40,48},{48,56},{56,64},{64,7... | collective-permute-start | bytes 1572872 | tf_op jit(solution)/shard_map/ppermute | solution.py:28
  11.8 24.4 %copy-start.2 = (bf16[1,2048,128]{2,1,0:T(8,128)(2,1)S(1)}, bf16[1,2048,128]{2,1,0:T(8,128)(2,1)}, u32[]{:S(2)}) copy-start(bf16[1,2048,128]{2,1,0:T(8,128)(2,1)} %param.6) | copy-start | bytes 1572868
  22.3 13.9 %copy-start = (f32[1,2048,128]{2,1,0:T(8,128)S(1)}, f32[1,2048,128]{2,1,0:T(8,128)}, u32[]{:S(2)}) copy-start(f32[1,2048,128]{2,1,0:T(8,128)} %param.8) | copy-start | bytes 3145732
  22.3 13.9 %copy-start.1 = (f32[1,2048,128]{2,1,0:T(8,128)S(1)}, f32[1,2048,128]{2,1,0:T(8,128)}, u32[]{:S(2)}) copy-start(f32[1,2048,128]{2,1,0:T(8,128)} %param.7) | copy-start | bytes 3145732
  23.4 13.7 %collective-permute-start.2 = (bf16[16,2432]{1,0:T(8,128)(2,1)S(1)}, bf16[16,2432]{1,0:T(8,128)(2,1)S(1)}, u32[]{:S(2)}, u32[]{:S(2)}) collective-permute-start(bf16[16,2432]{1,0:T(8,128)(2,1)S(1)} %image.1.left_ref), channel_id=1, source_target_pairs={{0,504},{8,0},{16,8},{24,16},{32,24},{40,32},{48,40},{56,48},{64,5... | collective-permute-start | bytes 233480 | tf_op jit(solution)/shard_map/ppermute | solution.py:28

commit v4 on v3

--- a/solution.py
+++ b/solution.py
@@ -180,7 +180,8 @@
         left_product,
         w_here,
     )
-    gathered = lax.all_to_all(partials, "tensor", 0, 0)
+    order = list(range(peers // 2)) + list(range(peers - 1, peers // 2 - 1, -1))
+    gathered = lax.all_to_all(partials, "tensor", 0, 0, axis_index_groups=[order])
     basis = call(basis_kernel, "basis", shaped((rank, rows), bf16), gathered)
     pack = call(
         image_kernel, "image", shaped((rank, rows + 3 * cols), bf16), basis, w_left, w_here

time: 38.5 us -> 38.2 us (level)
  waiting for transfers between devices: 1.49 us -> 1.9 us
  blocking collectives: 10.5 us -> 10.1 us
    ppermute x3, waiting for transfers between devices: 1.49 us -> 1.9 us  [shifted(): return lax.ppermute(value, axis, pairs)]
  transfers between devices with their start and end apart: 3 -> 3, of which waited for: 1 -> 2; matrix products, arithmetic and copies ran while one was open for 2% -> 2% of each run, Pallas kernels for 3% -> 3%
where the time goes in v4:
time: 38.2 us; the launch traced here: 38 us
  starting transfers between devices  20.7 us (54%)
  blocking collectives  10.1 us (26%)
  Pallas kernels  3.65 us (10%)
  waiting for transfers between devices  1.9 us (5%)
  other arithmetic  0.87 us (2%)
  between operations  0.72 us (2%)
    ppermute x3, starting transfers between devices, shifted(): return lax.ppermute(value, axis, pairs)  20.7 us
    all_to_all x1, blocking collectives, body(): lax.all_to_all(partials, 'tensor', 0, 0, axis_index_groups=[order])  10.1 us
    ppermute x3, waiting for transfers between devices, shifted(): return lax.ppermute(value, axis, pairs)  1.9 us
    pallas_call x1, Pallas kernels, body(): pl.pallas_call(product_kernel, out_shape=(pltpu.VMEM((rank, rows + cols),...  1.31 us
    pallas_call x3, Pallas kernels, call(): pl.pallas_call(kernel, out_shape=out_shape, in_specs=[vmem] * len(operand...  1.25 us
    pallas_call x1, Pallas kernels, body(): pl.pallas_call(update_kernel, out_shape=(shaped((rows, cols), bf16), shap...  1.09 us
    sub x1, other arithmetic, body(): pre = wide - learn_rate * step  0.87 us
  transfers between devices with their start and end apart: 3, of which 2 were waited for; matrix products, arithmetic and copies ran while one was open for 2% of the time, Pallas kernels for 3%

profile of v4, /device:TPU:1, one launch (start us, length us, event | category | flops | bytes accessed | tf_op | source)
XLA Modules:
  0.0 38.0 jit_solution(14176282066839995218)
XLA Ops:
  0.6 1.3 %own_product.1 = (f32[16,2176]{1,0:T(8,128)S(1)}, bf16[2048,128]{1,0:T(8,128)(2,1)S(1)}) custom-call(bf16[2048,128]{1,0:T(8,128)(2,1)} %bitcast.11, bf16[16,128]{1,0:T(8,128)(2,1)} %bitcast.12), custom_call_target="tpu_custom_call" | custom-call | flops 10000000 | bytes 4000000 | tf_op jit(solution)/shard_map/own_product/pallas_call | solution.py:156
  1.9 6.2 %collective-permute-start = (f32[16,2176]{1,0:T(8,128)S(1)}, f32[16,2176]{1,0:T(8,128)S(1)}, u32[]{:S(2)}, u32[]{:S(2)}) collective-permute-start(f32[16,2176]{1,0:T(8,128)S(1)} %get-tuple-element.6), channel_id=1, source_target_pairs={{0,8},{8,16},{16,24},{24,32},{32,40},{40,48},{48,56},{56,64},{64,7... | collective-permute-start | bytes 417800 | tf_op jit(solution)/shard_map/ppermute | solution.py:28
  8.2 1.9 %collective-permute-start.1 = (bf16[2048,128]{1,0:T(8,128)(2,1)S(1)}, bf16[2048,128]{1,0:T(8,128)(2,1)S(1)}, u32[]{:S(2)}, u32[]{:S(2)}) collective-permute-start(bf16[2048,128]{1,0:T(8,128)(2,1)S(1)} %get-tuple-element.7.w_ref), channel_id=1, source_target_pairs={{0,8},{8,16},{16,24},{24,32},{32,40},{40,48},{48,56},{56,64},{64,7... | collective-permute-start | bytes 1572872 | tf_op jit(solution)/shard_map/ppermute | solution.py:28
  10.1 1.5 %collective-permute-done.pack_ref = f32[16,2176]{1,0:T(8,128)S(1)} collective-permute-done((f32[16,2176]{1,0:T(8,128)S(1)}, f32[16,2176]{1,0:T(8,128)S(1)}, u32[]{:S(2)}, u32[]{:S(2)}) %collective-permute-start) | collective-permute-done | bytes 139296 | tf_op jit(solution)/shard_map/ppermute | solution.py:28
  11.6 0.3 partial_differences.1
  11.8 0.0 copy-start.2
  11.9 10.1 %all_to_all.5.g_ref = bf16[8,16,2048]{2,1,0:T(8,128)(2,1)S(1)} all-to-all(bf16[8,16,2048]{2,1,0:T(8,128)(2,1)S(1)} %partial_differences.1), channel_id=1, replica_groups={{0,1,2,3,7,6,5,4},{8,9,10,11,15,14,13,12},{16,17,18,19,23,22,21,20},{24..., dimensions={0} | all-to-all | bytes 1048576 | tf_op jit(solution)/shard_map/all_to_all | solution.py:184
  22.0 0.0 copy-start
  22.0 0.0 copy-start.1
  22.0 0.7 %basis.1.basis_ref = bf16[16,2048]{1,0:T(8,128)(2,1)S(1)} custom-call(bf16[8,16,2048]{2,1,0:T(8,128)(2,1)S(1)} %all_to_all.5.g_ref), custom_call_target="tpu_custom_call" | custom-call | flops 10000000 | bytes 4000000 | tf_op jit(solution)/shard_map/basis/pallas_call | solution.py:144
  22.7 0.0 collective-permute-done.1.wl_ref
  22.7 0.3 image.1.left_ref
  23.0 12.5 %collective-permute-start.2 = (bf16[16,2432]{1,0:T(8,128)(2,1)S(1)}, bf16[16,2432]{1,0:T(8,128)(2,1)S(1)}, u32[]{:S(2)}, u32[]{:S(2)}) collective-permute-start(bf16[16,2432]{1,0:T(8,128)(2,1)S(1)} %image.1.left_ref), channel_id=1, source_target_pairs={{0,504},{8,0},{16,8},{24,16},{32,24},{40,32},{48,40},{56,48},{64,5... | collective-permute-start | bytes 233480 | tf_op jit(solution)/shard_map/ppermute | solution.py:28
  35.5 0.0 copy-done.2
  35.6 0.0 copy-done
  35.6 0.0 copy-done.1
  35.6 0.9 %convert_subtract_fusion.pre_ref = f32[2048,128]{1,0:T(8,128)S(1)} fusion(bf16[2048,128]{1,0:T(8,128)(2,1)S(1)} %get-tuple-element.7.w_ref, f32[1,2048,128]{2,1,0:T(8,128)S(1)} %copy-done, f32[1,2048,128]{2,1,0:T(8,128)S(1)} %copy-done.1, bf16[1,2048,128]{2,1,0:T(8,128)(2,1)S(1)} %copy-done.2), kind=kLoop, calls=%fused_computation.3 | loop fusion | flops 4456448 | bytes 4194304 | tf_op jit(solution)/shard_map/sub | solution.py:196
  36.4 0.4 %collective-permute-done.2.right_ref = bf16[16,2432]{1,0:T(8,128)(2,1)S(1)} collective-permute-done((bf16[16,2432]{1,0:T(8,128)(2,1)S(1)}, bf16[16,2432]{1,0:T(8,128)(2,1)S(1)}, u32[]{:S(2)}, u32[]{:S(2)}) %collective-permute-start.2) | collective-permute-done | bytes 77856 | tf_op jit(solution)/shard_map/ppermute | solution.py:28
  36.9 1.1 %update.1 = (bf16[2048,128]{1,0:T(8,128)(2,1)}, f32[16,128]{1,0:T(8,128)}) custom-call(bf16[16,2432]{1,0:T(8,128)(2,1)S(1)} %image.1.left_ref, bf16[16,2432]{1,0:T(8,128)(2,1)S(1)} %collective-permute-done.2.right_ref, f32[2048,128]{1,0:T(8,128)S(1)} %convert_subtract_fusion.pre_ref), custom_call_target="tpu_custom_call" | custom-call | flops 10000000 | bytes 4000000 | tf_op jit(solution)/shard_map/update/pallas_call | solution.py:198
Async XLA Ops:
  1.9 9.6 %collective-permute-start = (f32[16,2176]{1,0:T(8,128)S(1)}, f32[16,2176]{1,0:T(8,128)S(1)}, u32[]{:S(2)}, u32[]{:S(2)}) collective-permute-start(f32[16,2176]{1,0:T(8,128)S(1)} %get-tuple-element.6), channel_id=1, source_target_pairs={{0,8},{8,16},{16,24},{24,32},{32,40},{40,48},{48,56},{56,64},{64,7... | collective-permute-start | bytes 417800 | tf_op jit(solution)/shard_map/ppermute | solution.py:28
  8.2 14.6 %collective-permute-start.1 = (bf16[2048,128]{1,0:T(8,128)(2,1)S(1)}, bf16[2048,128]{1,0:T(8,128)(2,1)S(1)}, u32[]{:S(2)}, u32[]{:S(2)}) collective-permute-start(bf16[2048,128]{1,0:T(8,128)(2,1)S(1)} %get-tuple-element.7.w_ref), channel_id=1, source_target_pairs={{0,8},{8,16},{16,24},{24,32},{32,40},{40,48},{48,56},{56,64},{64,7... | collective-permute-start | bytes 1572872 | tf_op jit(solution)/shard_map/ppermute | solution.py:28
  11.8 23.7 %copy-start.2 = (bf16[1,2048,128]{2,1,0:T(8,128)(2,1)S(1)}, bf16[1,2048,128]{2,1,0:T(8,128)(2,1)}, u32[]{:S(2)}) copy-start(bf16[1,2048,128]{2,1,0:T(8,128)(2,1)} %param.6) | copy-start | bytes 1572868
  22.0 13.6 %copy-start = (f32[1,2048,128]{2,1,0:T(8,128)S(1)}, f32[1,2048,128]{2,1,0:T(8,128)}, u32[]{:S(2)}) copy-start(f32[1,2048,128]{2,1,0:T(8,128)} %param.8) | copy-start | bytes 3145732
  22.0 13.6 %copy-start.1 = (f32[1,2048,128]{2,1,0:T(8,128)S(1)}, f32[1,2048,128]{2,1,0:T(8,128)}, u32[]{:S(2)}) copy-start(f32[1,2048,128]{2,1,0:T(8,128)} %param.7) | copy-start | bytes 3145732
  23.0 13.9 %collective-permute-start.2 = (bf16[16,2432]{1,0:T(8,128)(2,1)S(1)}, bf16[16,2432]{1,0:T(8,128)(2,1)S(1)}, u32[]{:S(2)}, u32[]{:S(2)}) collective-permute-start(bf16[16,2432]{1,0:T(8,128)(2,1)S(1)} %image.1.left_ref), channel_id=1, source_target_pairs={{0,504},{8,0},{16,8},{24,16},{32,24},{40,32},{48,40},{56,48},{64,5... | collective-permute-start | bytes 233480 | tf_op jit(solution)/shard_map/ppermute | solution.py:28

commit v5 on v4

--- a/solution.py
+++ b/solution.py
@@ -106,21 +106,33 @@
         image = image - piece.astype(f32)
 
 
-def update_kernel(left_ref, right_ref, pre_ref, new_hbm, next_hbm, new_ref, next_ref, sems):
-    width, cols = new_ref.shape
-    terms = [pl.ds(width + term * cols, cols) for term in range(3)]
-    pieces = [right_ref[:, t] for t in terms]
-    next_ref[...] = (
-        pieces[0].astype(f32) + pieces[1].astype(f32) + pieces[2].astype(f32)
-    )
-    copies = [pltpu.make_async_copy(next_ref, next_hbm, sems.at[0])]
-    copies[0].start()
-    nexts = jnp.concatenate(pieces + [-left_ref[:, t] for t in terms], 0)
+def left_kernel(left_ref, pre_ref, out_ref):
+    width, cols = out_ref.shape
+    nexts = jnp.concatenate(
+        [left_ref[:, pl.ds(width + term * cols, cols)] for term in range(3)], 0
+    )
     tile = 512
     for start in range(0, width, tile):
         rows = pl.ds(start, tile)
-        left, right = left_ref[:, rows], right_ref[:, rows]
-        lhs = jnp.concatenate([right, right, right, left, left, left], 0)
+        left = left_ref[:, rows]
+        lhs = jnp.concatenate([left, left, left], 0)
+        out_ref[rows] = pre_ref[rows] + gossip_rate * dot(lhs, nexts, ((0,), (0,)))
+
+
+def update_kernel(right_ref, pre_ref, new_hbm, next_hbm, new_ref, next_ref, sems):
+    width, cols = new_ref.shape
+    pieces = [right_ref[:, pl.ds(width + term * cols, cols)] for term in range(3)]
+    next_ref[...] = (
+        pieces[0].astype(f32) + pieces[1].astype(f32) + pieces[2].astype(f32)
+    )
+    copies = [pltpu.make_async_copy(next_ref, next_hbm, sems.at[0])]
+    copies[0].start()
+    nexts = jnp.concatenate(pieces, 0)
+    tile = 512
+    for start in range(0, width, tile):
+        rows = pl.ds(start, tile)
+        right = right_ref[:, rows]
+        lhs = jnp.concatenate([right, right, right], 0)
         correction = dot(lhs, nexts, ((0,), (0,)))
         new_ref[rows] = (pre_ref[rows] - gossip_rate * correction).astype(bf16)
         copies.append(
@@ -195,10 +207,11 @@
     step = first / bias_one / (jnp.sqrt(second / bias_two) + epsilon) + decay_rate * wide
     pre = wide - learn_rate * step
 
+    pre = call(left_kernel, "left_correction", shaped((rows, cols), f32), pack, pre)
     new, next_right = pl.pallas_call(
         update_kernel,
         out_shape=(shaped((rows, cols), bf16), shaped((rank, cols), f32)),
-        in_specs=[vmem] * 3,
+        in_specs=[vmem] * 2,
         out_specs=(hbm, hbm),
         scratch_shapes=[
             pltpu.VMEM((rows, cols), bf16),
@@ -210,7 +223,7 @@
             flops=10_000_000, bytes_accessed=4_000_000, transcendentals=0
         ),
         name="update",
-    )(pack, right_pack, pre)
+    )(right_pack, pre)
     return (new[None], next_right[None])
 
 

time: 38.2 us -> 38.2 us (level)
    pallas_call x3 -> x4, Pallas kernels: 1.25 us -> 1.59 us  [call(): pl.pallas_call(kernel, out_shape=out_shape, in_specs=[vmem] * len(operand...]
where the time goes in v5:
time: 38.2 us; the launch traced here: 38 us
  starting transfers between devices  20.7 us (54%)
  blocking collectives  10.1 us (26%)
  Pallas kernels  4.01 us (10%)
  waiting for transfers between devices  1.55 us (4%)
  other arithmetic  0.87 us (2%)
  between operations  0.73 us (2%)
    ppermute x3, starting transfers between devices, shifted(): return lax.ppermute(value, axis, pairs)  20.7 us
    all_to_all x1, blocking collectives, body(): lax.all_to_all(partials, 'tensor', 0, 0, axis_index_groups=[order])  10.1 us
    pallas_call x4, Pallas kernels, call(): pl.pallas_call(kernel, out_shape=out_shape, in_specs=[vmem] * len(operand...  1.59 us
    ppermute x3, waiting for transfers between devices, shifted(): return lax.ppermute(value, axis, pairs)  1.55 us
    pallas_call x1, Pallas kernels, body(): pl.pallas_call(product_kernel, out_shape=(pltpu.VMEM((rank, rows + cols),...  1.31 us
    pallas_call x1, Pallas kernels, body(): pl.pallas_call(update_kernel, out_shape=(shaped((rows, cols), bf16), shap...  1.11 us
    sub x1, other arithmetic, body(): pre = wide - learn_rate * step  0.87 us
  transfers between devices with their start and end apart: 3, of which 2 were waited for; matrix products, arithmetic and copies ran while one was open for 2% of the time, Pallas kernels for 3%

profile of v5, /device:TPU:1, one launch (start us, length us, event | category | flops | bytes accessed | tf_op | source)
XLA Modules:
  0.0 38.0 jit_solution(3772091305523188581)
XLA Ops:
  0.6 1.3 %own_product.1 = (f32[16,2176]{1,0:T(8,128)S(1)}, bf16[2048,128]{1,0:T(8,128)(2,1)S(1)}) custom-call(bf16[2048,128]{1,0:T(8,128)(2,1)} %bitcast.11, bf16[16,128]{1,0:T(8,128)(2,1)} %bitcast.12), custom_call_target="tpu_custom_call" | custom-call | flops 10000000 | bytes 4000000 | tf_op jit(solution)/shard_map/own_product/pallas_call | solution.py:168
  1.9 6.2 %collective-permute-start = (f32[16,2176]{1,0:T(8,128)S(1)}, f32[16,2176]{1,0:T(8,128)S(1)}, u32[]{:S(2)}, u32[]{:S(2)}) collective-permute-start(f32[16,2176]{1,0:T(8,128)S(1)} %get-tuple-element.6), channel_id=1, source_target_pairs={{0,8},{8,16},{16,24},{24,32},{32,40},{40,48},{48,56},{56,64},{64,7... | collective-permute-start | bytes 417800 | tf_op jit(solution)/shard_map/ppermute | solution.py:28
  8.2 1.9 %collective-permute-start.1 = (bf16[2048,128]{1,0:T(8,128)(2,1)S(1)}, bf16[2048,128]{1,0:T(8,128)(2,1)S(1)}, u32[]{:S(2)}, u32[]{:S(2)}) collective-permute-start(bf16[2048,128]{1,0:T(8,128)(2,1)S(1)} %get-tuple-element.7.w_ref), channel_id=1, source_target_pairs={{0,8},{8,16},{16,24},{24,32},{32,40},{40,48},{48,56},{56,64},{64,7... | collective-permute-start | bytes 1572872 | tf_op jit(solution)/shard_map/ppermute | solution.py:28
  10.1 1.5 %collective-permute-done.pack_ref = f32[16,2176]{1,0:T(8,128)S(1)} collective-permute-done((f32[16,2176]{1,0:T(8,128)S(1)}, f32[16,2176]{1,0:T(8,128)S(1)}, u32[]{:S(2)}, u32[]{:S(2)}) %collective-permute-start) | collective-permute-done | bytes 139296 | tf_op jit(solution)/shard_map/ppermute | solution.py:28
  11.6 0.3 partial_differences.1
  11.8 0.0 copy-start.2
  11.9 10.1 %all_to_all.5.g_ref = bf16[8,16,2048]{2,1,0:T(8,128)(2,1)S(1)} all-to-all(bf16[8,16,2048]{2,1,0:T(8,128)(2,1)S(1)} %partial_differences.1), channel_id=1, replica_groups={{0,1,2,3,7,6,5,4},{8,9,10,11,15,14,13,12},{16,17,18,19,23,22,21,20},{24..., dimensions={0} | all-to-all | bytes 1048576 | tf_op jit(solution)/shard_map/all_to_all | solution.py:196
  22.0 0.0 copy-start
  22.0 0.0 copy-start.1
  22.0 0.7 %basis.1.basis_ref = bf16[16,2048]{1,0:T(8,128)(2,1)S(1)} custom-call(bf16[8,16,2048]{2,1,0:T(8,128)(2,1)S(1)} %all_to_all.5.g_ref), custom_call_target="tpu_custom_call" | custom-call | flops 10000000 | bytes 4000000 | tf_op jit(solution)/shard_map/basis/pallas_call | solution.py:156
  22.7 0.0 collective-permute-done.1.wl_ref
  22.7 0.3 image.1.left_ref
  23.0 12.5 %collective-permute-start.2 = (bf16[16,2432]{1,0:T(8,128)(2,1)S(1)}, bf16[16,2432]{1,0:T(8,128)(2,1)S(1)}, u32[]{:S(2)}, u32[]{:S(2)}) collective-permute-start(bf16[16,2432]{1,0:T(8,128)(2,1)S(1)} %image.1.left_ref), channel_id=1, source_target_pairs={{0,504},{8,0},{16,8},{24,16},{32,24},{40,32},{48,40},{56,48},{64,5... | collective-permute-start | bytes 233480 | tf_op jit(solution)/shard_map/ppermute | solution.py:28
  35.5 0.0 copy-done.2
  35.6 0.0 copy-done
  35.6 0.0 copy-done.1
  35.6 0.9 %convert_subtract_fusion.pre_ref = f32[2048,128]{1,0:T(8,128)S(1)} fusion(bf16[2048,128]{1,0:T(8,128)(2,1)S(1)} %get-tuple-element.7.w_ref, f32[1,2048,128]{2,1,0:T(8,128)S(1)} %copy-done, f32[1,2048,128]{2,1,0:T(8,128)S(1)} %copy-done.1, bf16[1,2048,128]{2,1,0:T(8,128)(2,1)S(1)} %copy-done.2), kind=kLoop, calls=%fused_computation.3 | loop fusion | flops 4456448 | bytes 4194304 | tf_op jit(solution)/shard_map/sub | solution.py:208
  36.4 0.3 left_correction.1.pre_ref
  36.8 0.1 collective-permute-done.2.right_ref
  36.9 1.1 %update.1 = (bf16[2048,128]{1,0:T(8,128)(2,1)}, f32[16,128]{1,0:T(8,128)}) custom-call(bf16[16,2432]{1,0:T(8,128)(2,1)S(1)} %collective-permute-done.2.right_ref, f32[2048,128]{1,0:T(8,128)S(1)} %left_correction.1.pre_ref), custom_call_target="tpu_custom_call" | custom-call | flops 10000000 | bytes 4000000 | tf_op jit(solution)/shard_map/update/pallas_call | solution.py:211
Async XLA Ops:
  1.9 9.6 %collective-permute-start = (f32[16,2176]{1,0:T(8,128)S(1)}, f32[16,2176]{1,0:T(8,128)S(1)}, u32[]{:S(2)}, u32[]{:S(2)}) collective-permute-start(f32[16,2176]{1,0:T(8,128)S(1)} %get-tuple-element.6), channel_id=1, source_target_pairs={{0,8},{8,16},{16,24},{24,32},{32,40},{40,48},{48,56},{56,64},{64,7... | collective-permute-start | bytes 417800 | tf_op jit(solution)/shard_map/ppermute | solution.py:28
  8.2 14.6 %collective-permute-start.1 = (bf16[2048,128]{1,0:T(8,128)(2,1)S(1)}, bf16[2048,128]{1,0:T(8,128)(2,1)S(1)}, u32[]{:S(2)}, u32[]{:S(2)}) collective-permute-start(bf16[2048,128]{1,0:T(8,128)(2,1)S(1)} %get-tuple-element.7.w_ref), channel_id=1, source_target_pairs={{0,8},{8,16},{16,24},{24,32},{32,40},{40,48},{48,56},{56,64},{64,7... | collective-permute-start | bytes 1572872 | tf_op jit(solution)/shard_map/ppermute | solution.py:28
  11.8 23.7 %copy-start.2 = (bf16[1,2048,128]{2,1,0:T(8,128)(2,1)S(1)}, bf16[1,2048,128]{2,1,0:T(8,128)(2,1)}, u32[]{:S(2)}) copy-start(bf16[1,2048,128]{2,1,0:T(8,128)(2,1)} %param.6) | copy-start | bytes 1572868
  22.0 13.6 %copy-start = (f32[1,2048,128]{2,1,0:T(8,128)S(1)}, f32[1,2048,128]{2,1,0:T(8,128)}, u32[]{:S(2)}) copy-start(f32[1,2048,128]{2,1,0:T(8,128)} %param.8) | copy-start | bytes 3145732
  22.0 13.6 %copy-start.1 = (f32[1,2048,128]{2,1,0:T(8,128)S(1)}, f32[1,2048,128]{2,1,0:T(8,128)}, u32[]{:S(2)}) copy-start(f32[1,2048,128]{2,1,0:T(8,128)} %param.7) | copy-start | bytes 3145732
  23.0 13.9 %collective-permute-start.2 = (bf16[16,2432]{1,0:T(8,128)(2,1)S(1)}, bf16[16,2432]{1,0:T(8,128)(2,1)S(1)}, u32[]{:S(2)}, u32[]{:S(2)}) collective-permute-start(bf16[16,2432]{1,0:T(8,128)(2,1)S(1)} %image.1.left_ref), channel_id=1, source_target_pairs={{0,504},{8,0},{16,8},{24,16},{32,24},{40,32},{48,40},{56,48},{64,5... | collective-permute-start | bytes 233480 | tf_op jit(solution)/shard_map/ppermute | solution.py:28

commit v6 on v5

--- a/solution.py
+++ b/solution.py
@@ -192,7 +192,7 @@
         left_product,
         w_here,
     )
-    order = list(range(peers // 2)) + list(range(peers - 1, peers // 2 - 1, -1))
+    order = [0, 1, 5, 4, 7, 6, 2, 3]
     gathered = lax.all_to_all(partials, "tensor", 0, 0, axis_index_groups=[order])
     basis = call(basis_kernel, "basis", shaped((rank, rows), bf16), gathered)
     pack = call(

time: 38.2 us -> 38.5 us (level)
  blocking collectives: 10.1 us -> 10.5 us
  transfers between devices with their start and end apart: 3 -> 3, of which waited for: 2 -> 1; matrix products, arithmetic and copies ran while one was open for 2% -> 2% of each run, Pallas kernels for 3% -> 3%
where the time goes in v6:
time: 38.5 us; the launch traced here: 38.3 us
  starting transfers between devices  20.7 us (54%)
  blocking collectives  10.5 us (27%)
  Pallas kernels  4.01 us (10%)
  waiting for transfers between devices  1.49 us (4%)
  other arithmetic  0.87 us (2%)
  between operations  0.74 us (2%)
    ppermute x3, starting transfers between devices, shifted(): return lax.ppermute(value, axis, pairs)  20.7 us
    all_to_all x1, blocking collectives, body(): lax.all_to_all(partials, 'tensor', 0, 0, axis_index_groups=[order])  10.5 us
    pallas_call x4, Pallas kernels, call(): pl.pallas_call(kernel, out_shape=out_shape, in_specs=[vmem] * len(operand...  1.59 us
    ppermute x3, waiting for transfers between devices, shifted(): return lax.ppermute(value, axis, pairs)  1.49 us
    pallas_call x1, Pallas kernels, body(): pl.pallas_call(product_kernel, out_shape=(pltpu.VMEM((rank, rows + cols),...  1.31 us
    pallas_call x1, Pallas kernels, body(): pl.pallas_call(update_kernel, out_shape=(shaped((rows, cols), bf16), shap...  1.11 us
    sub x1, other arithmetic, body(): pre = wide - learn_rate * step  0.87 us
  transfers between devices with their start and end apart: 3, of which 1 were waited for; matrix products, arithmetic and copies ran while one was open for 2% of the time, Pallas kernels for 3%

profile of v6, /device:TPU:1, one launch (start us, length us, event | category | flops | bytes accessed | tf_op | source)
XLA Modules:
  0.0 38.3 jit_solution(2929446801897913766)
XLA Ops:
  0.6 1.3 %own_product.1 = (f32[16,2176]{1,0:T(8,128)S(1)}, bf16[2048,128]{1,0:T(8,128)(2,1)S(1)}) custom-call(bf16[2048,128]{1,0:T(8,128)(2,1)} %bitcast.11, bf16[16,128]{1,0:T(8,128)(2,1)} %bitcast.12), custom_call_target="tpu_custom_call" | custom-call | flops 10000000 | bytes 4000000 | tf_op jit(solution)/shard_map/own_product/pallas_call | solution.py:168
  1.9 6.2 %collective-permute-start = (f32[16,2176]{1,0:T(8,128)S(1)}, f32[16,2176]{1,0:T(8,128)S(1)}, u32[]{:S(2)}, u32[]{:S(2)}) collective-permute-start(f32[16,2176]{1,0:T(8,128)S(1)} %get-tuple-element.6), channel_id=1, source_target_pairs={{0,8},{8,16},{16,24},{24,32},{32,40},{40,48},{48,56},{56,64},{64,7... | collective-permute-start | bytes 417800 | tf_op jit(solution)/shard_map/ppermute | solution.py:28
  8.2 1.9 %collective-permute-start.1 = (bf16[2048,128]{1,0:T(8,128)(2,1)S(1)}, bf16[2048,128]{1,0:T(8,128)(2,1)S(1)}, u32[]{:S(2)}, u32[]{:S(2)}) collective-permute-start(bf16[2048,128]{1,0:T(8,128)(2,1)S(1)} %get-tuple-element.7.w_ref), channel_id=1, source_target_pairs={{0,8},{8,16},{16,24},{24,32},{32,40},{40,48},{48,56},{56,64},{64,7... | collective-permute-start | bytes 1572872 | tf_op jit(solution)/shard_map/ppermute | solution.py:28
  10.1 1.5 %collective-permute-done.pack_ref = f32[16,2176]{1,0:T(8,128)S(1)} collective-permute-done((f32[16,2176]{1,0:T(8,128)S(1)}, f32[16,2176]{1,0:T(8,128)S(1)}, u32[]{:S(2)}, u32[]{:S(2)}) %collective-permute-start) | collective-permute-done | bytes 139296 | tf_op jit(solution)/shard_map/ppermute | solution.py:28
  11.6 0.3 partial_differences.1
  11.8 0.0 copy-start.2
  11.9 10.5 %all_to_all.5.g_ref = bf16[8,16,2048]{2,1,0:T(8,128)(2,1)S(1)} all-to-all(bf16[8,16,2048]{2,1,0:T(8,128)(2,1)S(1)} %partial_differences.1), channel_id=1, replica_groups={{0,1,5,4,7,6,2,3},{8,9,13,12,15,14,10,11},{16,17,21,20,23,22,18,19},{24..., dimensions={0} | all-to-all | bytes 1048576 | tf_op jit(solution)/shard_map/all_to_all | solution.py:196
  22.3 0.0 copy-start
  22.3 0.0 copy-start.1
  22.3 0.7 %basis.1.basis_ref = bf16[16,2048]{1,0:T(8,128)(2,1)S(1)} custom-call(bf16[8,16,2048]{2,1,0:T(8,128)(2,1)S(1)} %all_to_all.5.g_ref), custom_call_target="tpu_custom_call" | custom-call | flops 10000000 | bytes 4000000 | tf_op jit(solution)/shard_map/basis/pallas_call | solution.py:156
  23.1 0.0 collective-permute-done.1.wl_ref
  23.1 0.3 image.1.left_ref
  23.4 12.5 %collective-permute-start.2 = (bf16[16,2432]{1,0:T(8,128)(2,1)S(1)}, bf16[16,2432]{1,0:T(8,128)(2,1)S(1)}, u32[]{:S(2)}, u32[]{:S(2)}) collective-permute-start(bf16[16,2432]{1,0:T(8,128)(2,1)S(1)} %image.1.left_ref), channel_id=1, source_target_pairs={{0,504},{8,0},{16,8},{24,16},{32,24},{40,32},{48,40},{56,48},{64,5... | collective-permute-start | bytes 233480 | tf_op jit(solution)/shard_map/ppermute | solution.py:28
  35.9 0.0 copy-done.2
  35.9 0.0 copy-done
  35.9 0.0 copy-done.1
  35.9 0.9 %convert_subtract_fusion.pre_ref = f32[2048,128]{1,0:T(8,128)S(1)} fusion(bf16[2048,128]{1,0:T(8,128)(2,1)S(1)} %get-tuple-element.7.w_ref, f32[1,2048,128]{2,1,0:T(8,128)S(1)} %copy-done, f32[1,2048,128]{2,1,0:T(8,128)S(1)} %copy-done.1, bf16[1,2048,128]{2,1,0:T(8,128)(2,1)S(1)} %copy-done.2), kind=kLoop, calls=%fused_computation.3 | loop fusion | flops 4456448 | bytes 4194304 | tf_op jit(solution)/shard_map/sub | solution.py:208
  36.8 0.3 left_correction.1.pre_ref
  37.1 0.0 collective-permute-done.2.right_ref
  37.2 1.1 %update.1 = (bf16[2048,128]{1,0:T(8,128)(2,1)}, f32[16,128]{1,0:T(8,128)}) custom-call(bf16[16,2432]{1,0:T(8,128)(2,1)S(1)} %collective-permute-done.2.right_ref, f32[2048,128]{1,0:T(8,128)S(1)} %left_correction.1.pre_ref), custom_call_target="tpu_custom_call" | custom-call | flops 10000000 | bytes 4000000 | tf_op jit(solution)/shard_map/update/pallas_call | solution.py:211
Async XLA Ops:
  1.9 9.6 %collective-permute-start = (f32[16,2176]{1,0:T(8,128)S(1)}, f32[16,2176]{1,0:T(8,128)S(1)}, u32[]{:S(2)}, u32[]{:S(2)}) collective-permute-start(f32[16,2176]{1,0:T(8,128)S(1)} %get-tuple-element.6), channel_id=1, source_target_pairs={{0,8},{8,16},{16,24},{24,32},{32,40},{40,48},{48,56},{56,64},{64,7... | collective-permute-start | bytes 417800 | tf_op jit(solution)/shard_map/ppermute | solution.py:28
  8.2 14.9 %collective-permute-start.1 = (bf16[2048,128]{1,0:T(8,128)(2,1)S(1)}, bf16[2048,128]{1,0:T(8,128)(2,1)S(1)}, u32[]{:S(2)}, u32[]{:S(2)}) collective-permute-start(bf16[2048,128]{1,0:T(8,128)(2,1)S(1)} %get-tuple-element.7.w_ref), channel_id=1, source_target_pairs={{0,8},{8,16},{16,24},{24,32},{32,40},{40,48},{48,56},{56,64},{64,7... | collective-permute-start | bytes 1572872 | tf_op jit(solution)/shard_map/ppermute | solution.py:28
  11.8 24.1 %copy-start.2 = (bf16[1,2048,128]{2,1,0:T(8,128)(2,1)S(1)}, bf16[1,2048,128]{2,1,0:T(8,128)(2,1)}, u32[]{:S(2)}) copy-start(bf16[1,2048,128]{2,1,0:T(8,128)(2,1)} %param.6) | copy-start | bytes 1572868
  22.3 13.6 %copy-start = (f32[1,2048,128]{2,1,0:T(8,128)S(1)}, f32[1,2048,128]{2,1,0:T(8,128)}, u32[]{:S(2)}) copy-start(f32[1,2048,128]{2,1,0:T(8,128)} %param.8) | copy-start | bytes 3145732
  22.3 13.6 %copy-start.1 = (f32[1,2048,128]{2,1,0:T(8,128)S(1)}, f32[1,2048,128]{2,1,0:T(8,128)}, u32[]{:S(2)}) copy-start(f32[1,2048,128]{2,1,0:T(8,128)} %param.7) | copy-start | bytes 3145732
  23.4 13.8 %collective-permute-start.2 = (bf16[16,2432]{1,0:T(8,128)(2,1)S(1)}, bf16[16,2432]{1,0:T(8,128)(2,1)S(1)}, u32[]{:S(2)}, u32[]{:S(2)}) collective-permute-start(bf16[16,2432]{1,0:T(8,128)(2,1)S(1)} %image.1.left_ref), channel_id=1, source_target_pairs={{0,504},{8,0},{16,8},{24,16},{32,24},{40,32},{48,40},{56,48},{64,5... | collective-permute-start | bytes 233480 | tf_op jit(solution)/shard_map/ppermute | solution.py:28
